TPU v7x, 32 devices: a whole 2x2x4 slice. The times are simulated.
32 devices in a mesh: fsdp: 4 (over y, x), rep: 8 (over z, core).
Axes of the slice: x: 2, y: 2, z: 4, core: 2. Of those that a mesh axis runs over, the one named last changes fastest.
Arguments:
- inputs: bfloat16 [1, 28672, 1280], P(None, ('fsdp', 'rep')), may hold values from -6 to 6
- cotangent: bfloat16 [1, 28672, 1280], P(None, ('fsdp', 'rep')), may hold values from -6 to 6
- lengths: int32 [1, 32], replicated, may hold values from 560 to 896
- threshold: int32 [1], replicated, may hold values from 8 to 48
- w_query: bfloat16 [1280, 1280], P('fsdp'), may hold values from -1 to 1
- w_key: bfloat16 [1280, 1280], P('fsdp'), may hold values from -0.15625 to 0.15625
- w_value: bfloat16 [1280, 1280], P('fsdp'), may hold values from -0.15625 to 0.15625
- w_out: bfloat16 [1280, 1280], P('fsdp'), may hold values from -1.25 to 1.25
- w_up: bfloat16 [1280, 5120], P('fsdp'), may hold values from -0.15625 to 0.15625
- w_down: bfloat16 [5120, 1280], P('fsdp'), may hold values from -0.078125 to 0.078125
- b_query: bfloat16 [1280], P('fsdp'), may hold values from -1.75 to 1.75
- b_value: bfloat16 [1280], P('fsdp'), may hold values from -3 to 3
- b_out: bfloat16 [1280], P('fsdp'), may hold values from -3 to 3
- b_up: bfloat16 [5120], P('fsdp'), may hold values from -3 to 3
- b_down: bfloat16 [1280], P('fsdp'), may hold values from -3 to 3
- gain_attn: bfloat16 [1280], P('fsdp'), may hold values from 0.25 to 1.75
- shift_attn: bfloat16 [1280], P('fsdp'), may hold values from -1.75 to 1.75
- gain_ffn: bfloat16 [1280], P('fsdp'), may hold values from 0.25 to 1.75
- shift_ffn: bfloat16 [1280], P('fsdp'), may hold values from -1.75 to 1.75
Outputs:
- layer_out: bfloat16 [1, 28672, 1280], P(None, ('fsdp', 'rep'))
- grad_inputs: float32 [1, 28672, 1280], P(None, ('fsdp', 'rep'))
- grad_w_query: float32 [1280, 1280], P('fsdp')
- grad_w_key: float32 [1280, 1280], P('fsdp')
- grad_w_value: float32 [1280, 1280], P('fsdp')
- grad_w_out: float32 [1280, 1280], P('fsdp')
- grad_w_up: float32 [1280, 5120], P('fsdp')
- grad_w_down: float32 [5120, 1280], P('fsdp')
- grad_b_query: float32 [1280], P('fsdp')
- grad_b_value: float32 [1280], P('fsdp')
- grad_b_out: float32 [1280], P('fsdp')
- grad_b_up: float32 [5120], P('fsdp')
- grad_b_down: float32 [1280], P('fsdp')
- grad_gain_attn: float32 [1280], P('fsdp')
- grad_shift_attn: float32 [1280], P('fsdp')
- grad_gain_ffn: float32 [1280], P('fsdp')
- grad_shift_ffn: float32 [1280], P('fsdp')
- head_peak: float32 [16], replicated
- clip_factor: float32 [16], replicated
- clipped_query: bfloat16 [1280, 1280], P('fsdp')
- clipped_key: bfloat16 [1280, 1280], P('fsdp')
All inputs are finite; a program needn't handle non-finite values.
Results may differ from a plain program's by a relative error of at most 0.019.
Values may be sent and summed in bfloat16 or wider, within the bound.
No kernel may reach another device: no remote copies, remote signals or barrier semaphores. Data moves between devices by JAX's collectives and lax.ppermute only.
A program may use at most 320 MiB of HBM per device.

v0:
```python
import jax
import jax.numpy as jnp
from jax import lax
from jax.sharding import PartitionSpec as P

H = 16
HD = 80


epsilon = 1e-05
masked_value = -1e30
threshold_unit = 16.0


def layer_norm(values, gain_vec, shift_vec):
    centre = values - jnp.mean(values, axis=-1, keepdims=True)
    spread = jnp.mean(centre * centre, axis=-1, keepdims=True)
    return centre * lax.rsqrt(spread + epsilon) * gain_vec + shift_vec


def gelu_exact(values):
    return jax.nn.gelu(values, approximate=False)


def to_blocks(values, head_group):
    clip_count, length = (values.shape[0], values.shape[1])
    shaped = values.reshape(clip_count, length, H // head_group, head_group, HD)
    return shaped.transpose(0, 2, 1, 3, 4).reshape(
        clip_count * (H // head_group), length, head_group, HD
    )


def from_blocks(values, clip_count, head_group):
    length = values.shape[1]
    shaped = values.reshape(clip_count, H // head_group, length, head_group, HD)
    return shaped.transpose(0, 2, 1, 3, 4).reshape(clip_count, length, H * HD)


def block_scores(query_block, key_block, visible):
    raw_scores = jnp.einsum(
        "qge,kge->gqk", query_block, key_block, preferred_element_type=jnp.float32
    )
    return jnp.where(visible[None, None, :], raw_scores * HD ** (-0.5), masked_value)


def attend_forward(packed):
    query_block, key_block, value_block, visible = packed
    scores = block_scores(query_block, key_block, visible)
    row_peak = jnp.max(scores, axis=2, keepdims=True)
    expo_terms = jnp.exp(scores - row_peak)
    row_total = jnp.sum(expo_terms, axis=2, keepdims=True)
    probabilities = (expo_terms / row_total).astype(jnp.bfloat16)
    mixed_rows = jnp.einsum(
        "gqk,kge->qge", probabilities, value_block, preferred_element_type=jnp.float32
    )
    return (
        mixed_rows,
        (row_peak + jnp.log(row_total))[:, :, 0],
        jnp.max(row_peak[:, :, 0], axis=1),
    )


def attend_backward(packed):
    query_block, key_block, value_block, visible, log_total, grad_mixed = packed
    scores = block_scores(query_block, key_block, visible)
    probabilities = jnp.exp(scores - log_total[:, :, None])
    grad_probs = jnp.einsum(
        "qge,kge->gqk", grad_mixed, value_block, preferred_element_type=jnp.float32
    )
    inner_sum = jnp.sum(probabilities * grad_probs, axis=2, keepdims=True)
    grad_raw = (probabilities * (grad_probs - inner_sum) * HD ** (-0.5)).astype(jnp.bfloat16)
    grad_query = jnp.einsum("gqk,kge->qge", grad_raw, key_block, preferred_element_type=jnp.float32)
    grad_key = jnp.einsum("gqk,qge->kge", grad_raw, query_block, preferred_element_type=jnp.float32)
    grad_value = jnp.einsum(
        "gqk,qge->kge",
        probabilities.astype(jnp.bfloat16),
        grad_mixed,
        preferred_element_type=jnp.float32,
    )
    return (grad_query, grad_key, grad_value)


def column_sums(values):
    return jnp.sum(values.astype(jnp.float32), axis=0)


def per_device(
    inputs,
    cotangent,
    lengths,
    threshold,
    w_query,
    w_key,
    w_value,
    w_out,
    w_up,
    w_down,
    b_query,
    b_value,
    b_out,
    b_up,
    b_down,
    gain_attn,
    shift_attn,
    gain_ffn,
    shift_ffn,
):
    gathered = (
        lax.all_gather(w_query, "fsdp", axis=0, tiled=True),
        lax.all_gather(w_key, "fsdp", axis=0, tiled=True),
        lax.all_gather(w_value, "fsdp", axis=0, tiled=True),
        lax.all_gather(w_out, "fsdp", axis=0, tiled=True),
        lax.all_gather(w_up, "fsdp", axis=0, tiled=True),
        lax.all_gather(w_down, "fsdp", axis=0, tiled=True),
        lax.all_gather(b_query, "fsdp", axis=0, tiled=True),
        lax.all_gather(b_value, "fsdp", axis=0, tiled=True),
        lax.all_gather(b_out, "fsdp", axis=0, tiled=True),
        lax.all_gather(b_up, "fsdp", axis=0, tiled=True),
        lax.all_gather(b_down, "fsdp", axis=0, tiled=True),
        lax.all_gather(gain_attn, "fsdp", axis=0, tiled=True),
        lax.all_gather(shift_attn, "fsdp", axis=0, tiled=True),
        lax.all_gather(gain_ffn, "fsdp", axis=0, tiled=True),
        lax.all_gather(shift_ffn, "fsdp", axis=0, tiled=True),
    )
    (
        query_full,
        key_full,
        value_full,
        out_full,
        up_full,
        down_full,
        query_bias,
        value_bias,
        out_bias,
        up_bias,
        down_bias,
        attn_gain,
        attn_shift,
        ffn_gain,
        ffn_shift,
    ) = gathered
    attn_gain32 = attn_gain.astype(jnp.float32)
    attn_shift32 = attn_shift.astype(jnp.float32)
    ffn_gain32 = ffn_gain.astype(jnp.float32)
    ffn_shift32 = ffn_shift.astype(jnp.float32)
    clip_count, clip_length, feat_width = inputs.shape
    token_rows = clip_count * clip_length
    head_group = 4
    device_index = lax.axis_index("fsdp") * lax.axis_size("rep") + lax.axis_index("rep")
    valid_len = lax.dynamic_slice_in_dim(lengths, device_index, 1, 1)[:, 0]
    positions = jnp.arange(clip_length, dtype=jnp.int32)
    visible = positions[None, :] < valid_len[:, None]
    visible_blocks = jnp.repeat(visible, H // head_group, axis=0)
    frames = inputs.reshape(token_rows, feat_width).astype(jnp.float32)
    normed_low = layer_norm(frames, attn_gain32, attn_shift32).astype(jnp.bfloat16)
    queries = (
        jnp.dot(normed_low, query_full, preferred_element_type=jnp.float32)
        + query_bias.astype(jnp.float32)
    ).astype(jnp.bfloat16)
    key_rows = jnp.dot(normed_low, key_full, preferred_element_type=jnp.float32).astype(
        jnp.bfloat16
    )
    value_rows = (
        jnp.dot(normed_low, value_full, preferred_element_type=jnp.float32)
        + value_bias.astype(jnp.float32)
    ).astype(jnp.bfloat16)
    query_blocks = to_blocks(queries.reshape(clip_count, clip_length, feat_width), head_group)
    key_blocks = to_blocks(key_rows.reshape(clip_count, clip_length, feat_width), head_group)
    value_blocks = to_blocks(value_rows.reshape(clip_count, clip_length, feat_width), head_group)
    mixed_blocks, log_totals, peaks = lax.map(
        attend_forward, (query_blocks, key_blocks, value_blocks, visible_blocks)
    )
    head_local = jnp.max(peaks.reshape(clip_count, H), axis=0)
    head_peak = lax.pmax(head_local, ("fsdp", "rep"))
    mixed_low = (
        from_blocks(mixed_blocks, clip_count, head_group)
        .reshape(token_rows, feat_width)
        .astype(jnp.bfloat16)
    )
    middle = (
        frames
        + jnp.dot(mixed_low, out_full, preferred_element_type=jnp.float32)
        + out_bias.astype(jnp.float32)
    )
    ffn_low = layer_norm(middle, ffn_gain32, ffn_shift32).astype(jnp.bfloat16)
    before = jnp.dot(ffn_low, up_full, preferred_element_type=jnp.float32) + up_bias.astype(
        jnp.float32
    )
    hidden_low = gelu_exact(before).astype(jnp.bfloat16)
    result = (
        middle
        + jnp.dot(hidden_low, down_full, preferred_element_type=jnp.float32)
        + down_bias.astype(jnp.float32)
    )
    layer_out = result.astype(jnp.bfloat16).reshape(clip_count, clip_length, feat_width)
    grad_out_rows = cotangent.reshape(token_rows, feat_width).astype(jnp.float32)
    grad_down_low = cotangent.reshape(token_rows, feat_width)
    grad_w_down = jnp.einsum(
        "rf,rd->fd", hidden_low, grad_down_low, preferred_element_type=jnp.float32
    )
    grad_b_down = column_sums(grad_down_low)
    grad_hidden = jnp.einsum(
        "rd,fd->rf", grad_down_low, down_full, preferred_element_type=jnp.float32
    )
    _, gelu_pull = jax.vjp(gelu_exact, before)
    grad_before_low = gelu_pull(grad_hidden)[0].astype(jnp.bfloat16)
    grad_w_up = jnp.einsum(
        "rd,rf->df", ffn_low, grad_before_low, preferred_element_type=jnp.float32
    )
    grad_b_up = column_sums(grad_before_low)
    grad_normed_ffn = jnp.einsum(
        "rf,df->rd", grad_before_low, up_full, preferred_element_type=jnp.float32
    )
    _, second_pull = jax.vjp(layer_norm, middle, ffn_gain32, ffn_shift32)
    grad_middle_part, grad_gain_ffn, grad_shift_ffn = second_pull(grad_normed_ffn)
    grad_middle = grad_out_rows + grad_middle_part
    grad_attn_low = grad_middle.astype(jnp.bfloat16)
    grad_w_out = jnp.einsum(
        "rd,re->de", mixed_low, grad_attn_low, preferred_element_type=jnp.float32
    )
    grad_b_out = column_sums(grad_attn_low)
    grad_mixed = jnp.einsum(
        "re,de->rd", grad_attn_low, out_full, preferred_element_type=jnp.float32
    ).astype(jnp.bfloat16)
    grad_mixed_blocks = to_blocks(
        grad_mixed.reshape(clip_count, clip_length, feat_width), head_group
    )
    grad_q_blocks, grad_k_blocks, grad_v_blocks = lax.map(
        attend_backward,
        (query_blocks, key_blocks, value_blocks, visible_blocks, log_totals, grad_mixed_blocks),
    )
    grad_queries_low = (
        from_blocks(grad_q_blocks, clip_count, head_group)
        .reshape(token_rows, feat_width)
        .astype(jnp.bfloat16)
    )
    grad_keys_low = (
        from_blocks(grad_k_blocks, clip_count, head_group)
        .reshape(token_rows, feat_width)
        .astype(jnp.bfloat16)
    )
    grad_values_low = (
        from_blocks(grad_v_blocks, clip_count, head_group)
        .reshape(token_rows, feat_width)
        .astype(jnp.bfloat16)
    )
    grad_w_query = jnp.einsum(
        "rd,re->de", normed_low, grad_queries_low, preferred_element_type=jnp.float32
    )
    grad_w_key = jnp.einsum(
        "rd,re->de", normed_low, grad_keys_low, preferred_element_type=jnp.float32
    )
    grad_w_value = jnp.einsum(
        "rd,re->de", normed_low, grad_values_low, preferred_element_type=jnp.float32
    )
    grad_b_query = column_sums(grad_queries_low)
    grad_b_value = column_sums(grad_values_low)
    grad_normed = (
        jnp.einsum("re,de->rd", grad_queries_low, query_full, preferred_element_type=jnp.float32)
        + jnp.einsum("re,de->rd", grad_keys_low, key_full, preferred_element_type=jnp.float32)
        + jnp.einsum("re,de->rd", grad_values_low, value_full, preferred_element_type=jnp.float32)
    )
    _, first_pull = jax.vjp(layer_norm, frames, attn_gain32, attn_shift32)
    grad_frames_part, grad_gain_attn, grad_shift_attn = first_pull(grad_normed)
    grad_inputs = (grad_middle + grad_frames_part).reshape(clip_count, clip_length, feat_width)
    pieces = (
        lax.psum_scatter(
            grad_w_query.astype(jnp.bfloat16), "fsdp", scatter_dimension=0, tiled=True
        ).astype(jnp.float32),
        lax.psum_scatter(
            grad_w_key.astype(jnp.bfloat16), "fsdp", scatter_dimension=0, tiled=True
        ).astype(jnp.float32),
        lax.psum_scatter(
            grad_w_value.astype(jnp.bfloat16), "fsdp", scatter_dimension=0, tiled=True
        ).astype(jnp.float32),
        lax.psum_scatter(
            grad_w_out.astype(jnp.bfloat16), "fsdp", scatter_dimension=0, tiled=True
        ).astype(jnp.float32),
        lax.psum_scatter(
            grad_w_up.astype(jnp.bfloat16), "fsdp", scatter_dimension=0, tiled=True
        ).astype(jnp.float32),
        lax.psum_scatter(
            grad_w_down.astype(jnp.bfloat16), "fsdp", scatter_dimension=0, tiled=True
        ).astype(jnp.float32),
        lax.psum_scatter(
            grad_b_query.astype(jnp.bfloat16), "fsdp", scatter_dimension=0, tiled=True
        ).astype(jnp.float32),
        lax.psum_scatter(
            grad_b_value.astype(jnp.bfloat16), "fsdp", scatter_dimension=0, tiled=True
        ).astype(jnp.float32),
        lax.psum_scatter(
            grad_b_out.astype(jnp.bfloat16), "fsdp", scatter_dimension=0, tiled=True
        ).astype(jnp.float32),
        lax.psum_scatter(
            grad_b_up.astype(jnp.bfloat16), "fsdp", scatter_dimension=0, tiled=True
        ).astype(jnp.float32),
        lax.psum_scatter(
            grad_b_down.astype(jnp.bfloat16), "fsdp", scatter_dimension=0, tiled=True
        ).astype(jnp.float32),
        lax.psum_scatter(
            grad_gain_attn.astype(jnp.bfloat16), "fsdp", scatter_dimension=0, tiled=True
        ).astype(jnp.float32),
        lax.psum_scatter(
            grad_shift_attn.astype(jnp.bfloat16), "fsdp", scatter_dimension=0, tiled=True
        ).astype(jnp.float32),
        lax.psum_scatter(
            grad_gain_ffn.astype(jnp.bfloat16), "fsdp", scatter_dimension=0, tiled=True
        ).astype(jnp.float32),
        lax.psum_scatter(
            grad_shift_ffn.astype(jnp.bfloat16), "fsdp", scatter_dimension=0, tiled=True
        ).astype(jnp.float32),
    )
    shares = (
        lax.psum_scatter(
            pieces[0].astype(jnp.bfloat16), "rep", scatter_dimension=0, tiled=True
        ).astype(jnp.float32),
        lax.psum_scatter(
            pieces[1].astype(jnp.bfloat16), "rep", scatter_dimension=0, tiled=True
        ).astype(jnp.float32),
        lax.psum_scatter(
            pieces[2].astype(jnp.bfloat16), "rep", scatter_dimension=0, tiled=True
        ).astype(jnp.float32),
        lax.psum_scatter(
            pieces[3].astype(jnp.bfloat16), "rep", scatter_dimension=0, tiled=True
        ).astype(jnp.float32),
        lax.psum_scatter(
            pieces[4].astype(jnp.bfloat16), "rep", scatter_dimension=0, tiled=True
        ).astype(jnp.float32),
        lax.psum_scatter(
            pieces[5].astype(jnp.bfloat16), "rep", scatter_dimension=0, tiled=True
        ).astype(jnp.float32),
        lax.psum_scatter(
            pieces[6].astype(jnp.bfloat16), "rep", scatter_dimension=0, tiled=True
        ).astype(jnp.float32),
        lax.psum_scatter(
            pieces[7].astype(jnp.bfloat16), "rep", scatter_dimension=0, tiled=True
        ).astype(jnp.float32),
        lax.psum_scatter(
            pieces[8].astype(jnp.bfloat16), "rep", scatter_dimension=0, tiled=True
        ).astype(jnp.float32),
        lax.psum_scatter(
            pieces[9].astype(jnp.bfloat16), "rep", scatter_dimension=0, tiled=True
        ).astype(jnp.float32),
        lax.psum_scatter(
            pieces[10].astype(jnp.bfloat16), "rep", scatter_dimension=0, tiled=True
        ).astype(jnp.float32),
        lax.psum_scatter(
            pieces[11].astype(jnp.bfloat16), "rep", scatter_dimension=0, tiled=True
        ).astype(jnp.float32),
        lax.psum_scatter(
            pieces[12].astype(jnp.bfloat16), "rep", scatter_dimension=0, tiled=True
        ).astype(jnp.float32),
        lax.psum_scatter(
            pieces[13].astype(jnp.bfloat16), "rep", scatter_dimension=0, tiled=True
        ).astype(jnp.float32),
        lax.psum_scatter(
            pieces[14].astype(jnp.bfloat16), "rep", scatter_dimension=0, tiled=True
        ).astype(jnp.float32),
    )
    owned_grads = (
        lax.all_gather(shares[0].astype(jnp.bfloat16), "rep", axis=0, tiled=True).astype(
            jnp.float32
        ),
        lax.all_gather(shares[1].astype(jnp.bfloat16), "rep", axis=0, tiled=True).astype(
            jnp.float32
        ),
        lax.all_gather(shares[2].astype(jnp.bfloat16), "rep", axis=0, tiled=True).astype(
            jnp.float32
        ),
        lax.all_gather(shares[3].astype(jnp.bfloat16), "rep", axis=0, tiled=True).astype(
            jnp.float32
        ),
        lax.all_gather(shares[4].astype(jnp.bfloat16), "rep", axis=0, tiled=True).astype(
            jnp.float32
        ),
        lax.all_gather(shares[5].astype(jnp.bfloat16), "rep", axis=0, tiled=True).astype(
            jnp.float32
        ),
        lax.all_gather(shares[6].astype(jnp.bfloat16), "rep", axis=0, tiled=True).astype(
            jnp.float32
        ),
        lax.all_gather(shares[7].astype(jnp.bfloat16), "rep", axis=0, tiled=True).astype(
            jnp.float32
        ),
        lax.all_gather(shares[8].astype(jnp.bfloat16), "rep", axis=0, tiled=True).astype(
            jnp.float32
        ),
        lax.all_gather(shares[9].astype(jnp.bfloat16), "rep", axis=0, tiled=True).astype(
            jnp.float32
        ),
        lax.all_gather(shares[10].astype(jnp.bfloat16), "rep", axis=0, tiled=True).astype(
            jnp.float32
        ),
        lax.all_gather(shares[11].astype(jnp.bfloat16), "rep", axis=0, tiled=True).astype(
            jnp.float32
        ),
        lax.all_gather(shares[12].astype(jnp.bfloat16), "rep", axis=0, tiled=True).astype(
            jnp.float32
        ),
        lax.all_gather(shares[13].astype(jnp.bfloat16), "rep", axis=0, tiled=True).astype(
            jnp.float32
        ),
        lax.all_gather(shares[14].astype(jnp.bfloat16), "rep", axis=0, tiled=True).astype(
            jnp.float32
        ),
    )
    clip_limit = threshold[0].astype(jnp.float32) / threshold_unit
    factor = jnp.sqrt(clip_limit / jnp.maximum(head_peak, clip_limit))
    columns = jnp.repeat(factor, HD, total_repeat_length=H * HD)
    clipped_query = (w_query.astype(jnp.float32) * columns[None, :]).astype(jnp.bfloat16)
    clipped_key = (w_key.astype(jnp.float32) * columns[None, :]).astype(jnp.bfloat16)
    return (
        layer_out,
        grad_inputs,
        owned_grads[0],
        owned_grads[1],
        owned_grads[2],
        owned_grads[3],
        owned_grads[4],
        owned_grads[5],
        owned_grads[6],
        owned_grads[7],
        owned_grads[8],
        owned_grads[9],
        owned_grads[10],
        owned_grads[11],
        owned_grads[12],
        owned_grads[13],
        owned_grads[14],
        head_peak,
        factor,
        clipped_query,
        clipped_key,
    )


def solution(mesh):
    return jax.shard_map(
        per_device,
        mesh=mesh,
        in_specs=(
            P(None, ("fsdp", "rep"), None),
            P(None, ("fsdp", "rep"), None),
            P(),
            P(),
            P("fsdp", None),
            P("fsdp", None),
            P("fsdp", None),
            P("fsdp", None),
            P("fsdp", None),
            P("fsdp", None),
            P("fsdp"),
            P("fsdp"),
            P("fsdp"),
            P("fsdp"),
            P("fsdp"),
            P("fsdp"),
            P("fsdp"),
            P("fsdp"),
            P("fsdp"),
        ),
        out_specs=(
            P(None, ("fsdp", "rep"), None),
            P(None, ("fsdp", "rep"), None),
            P("fsdp", None),
            P("fsdp", None),
            P("fsdp", None),
            P("fsdp", None),
            P("fsdp", None),
            P("fsdp", None),
            P("fsdp"),
            P("fsdp"),
            P("fsdp"),
            P("fsdp"),
            P("fsdp"),
            P("fsdp"),
            P("fsdp"),
            P("fsdp"),
            P("fsdp"),
            P(),
            P(),
            P("fsdp", None),
            P("fsdp", None),
        ),
        check_vma=False,
    )
```

profile of v0, /device:TPU:0, one launch (start us, length us, event | category | flops | bytes accessed | tf_op | source)
XLA Modules:
  0.0 1315.5 jit_solution(2901858881312010569)
XLA Ops:
  69.2 35.8 %all-gather.12.cloned.1.call-done = bf16[1280,1280]{1,0:T(8,128)(2,1)} async-done(((bf16[320,1280]{1,0:T(8,128)(2,1)}), bf16[1280,1280]{1,0:T(8,128)(2,1)}) %all-gather.12.cloned.1.call-update) | async-done | bytes 3276816 | tf_op jit(solution)/shard_map/all_gather | solution.py:109
  116.2 35.8 %all-gather.14.cloned.1.call-done = bf16[1280,1280]{1,0:T(8,128)(2,1)} async-done(((bf16[320,1280]{1,0:T(8,128)(2,1)}), bf16[1280,1280]{1,0:T(8,128)(2,1)}) %all-gather.14.cloned.1.call-update) | async-done | bytes 3276816 | tf_op jit(solution)/shard_map/all_gather | solution.py:110
  164.6 66.9 %while.29 = (s32[]{:T(128)}, bf16[4,896,4,80]{1,3,2,0:T(8,128)(2,1)}, f32[4,4,896]{2,1,0:T(4,128)}, f32[4,4]{1,0:T(4,128)}, bf16[4,896,4,80]{1,3,2,0:T(8,128)(2,...) while((s32[]{:T(128)}, ...), condition=%wide.region_6.7_spmd, body=%wide.region_2.6_spmd.sunk | while | flops 1069347328 | bytes 59874516 | solution.py:170
  241.2 86.1 %all-gather.18.cloned.1.call-done = bf16[1280,5120]{1,0:T(8,128)(2,1)} async-done(((bf16[320,5120]{1,0:T(8,128)(2,1)}), bf16[1280,5120]{1,0:T(8,128)(2,1)}) %all-gather.18.cloned.1.call-update) | async-done | bytes 13107216 | tf_op jit(solution)/shard_map/all_gather | solution.py:113
  327.4 60.1 %multiply_convert_fusion.1 = (bf16[896,5120]{1,0:T(8,128)(2,1)}, f32[896,5120]{1,0:T(8,128)}, f32[896,5120]{1,0:T(8,128)}) fusion(f32[5120]{0:T(1024)S(1)} %bitcast.262, bf16[1280,5120]{1,0:T(8,128)(2,1)} %all-gather.18.cloned.1.call-done, f32[896,1280]{1,0:T(8,128)} %copy-done.7, f32[1280]{0:T(1024)S(1)} %copy-done.37, f32[1280]{0:T(1024)S(1)} %copy-done.31, ...), kind=kOutput, calls=%fused_computation.68 | convolution fusion | flops 12052561920 | bytes 63607808 | tf_op jit(solution)/shard_map/dot_general | solution.py:186
  387.5 68.5 %all-gather.20.cloned.1.call-done = bf16[5120,1280]{1,0:T(8,128)(2,1)} async-done(((bf16[1280,1280]{1,0:T(8,128)(2,1)}), bf16[5120,1280]{1,0:T(8,128)(2,1)}) %all-gather.20.cloned.1.call-update) | async-done | bytes 13107216 | tf_op jit(solution)/shard_map/all_gather | solution.py:114
  456.0 28.2 %fusion.122 = (bf16[5120]{0:T(1024)(128)(2,1)}, bf16[896,5120]{1,0:T(8,128)(2,1)}) fusion(f32[896,5120]{1,0:T(8,128)} %get-tuple-element.222, bf16[5120,1280]{1,0:T(8,128)(2,1)} %all-gather.20.cloned.1.call-done, bf16[1,896,1280]{2,1,0:T(8,128)(2,1)S(1)} %copy-done.5, f32[896,5120]{1,0:T(8,128)} %get-tuple-element.249, f32[5120]{0:T(1024)S(1)} %bitcast.263), kind=kOutput, calls=%fused_computation.154 | convolution fusion | flops 11817446400 | bytes 61306880 | tf_op jit(solution)/shard_map/rd,fd->rf/dot_general | solution.py:202
  484.2 21.1 %convolution_convert_fusion.1 = bf16[1280,5120]{1,0:T(8,128)(2,1)} fusion(bf16[896,5120]{1,0:T(8,128)(2,1)} %get-tuple-element.252, f32[896,1280]{1,0:T(8,128)} %copy-done.7, f32[1280]{0:T(1024)S(1)} %copy-done.37, f32[1280]{0:T(1024)S(1)} %copy-done.31, f32[896]{0:T(1024)S(1)} %fusion.104, f32[896]{0:T(1024)S(1)} %broadcast_multiply_fusion), kind=kOutput, calls=%fused_computation.65 | convolution fusion | flops 11756339200 | bytes 26887168 | tf_op jit(solution)/shard_map/rd,rf->df/dot_general | solution.py:207
  505.4 20.3 %convolution_convert_fusion = bf16[5120,1280]{1,0:T(8,128)(2,1)} fusion(bf16[896,5120]{1,0:T(8,128)(2,1)} %get-tuple-element.221, bf16[1,896,1280]{2,1,0:T(8,128)(2,1)S(1)} %copy-done.5), kind=kOutput, calls=%fused_computation.64 | convolution fusion | flops 11750604800 | bytes 24576000 | tf_op jit(solution)/shard_map/rf,rd->fd/dot_general | solution.py:198
  525.7 23.9 %multiply_reduce_fusion.1 = (bf16[1280]{0:T(1024)(128)(2,1)}, f32[896]{0:T(1024)S(1)}, bf16[1280]{0:T(1024)(128)(2,1)}, f32[896,1280]{1,0:T(8,128)}) fusion(f32[896,1280]{1,0:T(8,128)} %copy-done.7, f32[896]{0:T(1024)S(1)} %fusion.104, f32[896]{0:T(1024)S(1)} %broadcast_multiply_fusion, f32[1280]{0:T(1024)S(1)} %copy-done.31, ...), kind=kOutput, calls=%fused_computation.109 | convolution fusion | flops 11753223168 | bytes 31478272 | tf_op jit(solution)/shard_map/rf,df->rd/dot_general | solution.py:211
  580.3 265.4 %while.30 = (s32[]{:T(128)}, bf16[4,896,4,80]{1,3,2,0:T(8,128)(2,1)}, bf16[4,896,4,80]{1,3,2,0:T(8,128)(2,1)}, bf16[4,896,4,80]{1,3,2,0:T(8,128)(2,1)}, bf16[4,8...) while((s32[]{:T(128)}, ...), condition=%wide.region_13.14_spmd, body=%wide.region_11.13_spmd.sunk | while | flops 2613977856 | bytes 148801264 | solution.py:228
  598.4 19.9 %fusion.186 = bf16[4,896,4,80]{1,3,2,0:T(8,128)(2,1)} fusion(bf16[4,896,4,80]{1,3,2,0:T(8,128)(2,1)} %get-tuple-element.417, s32[]{:T(128)} %get-tuple-element.415, f32[4,896,896]{1,2,0:T(8,128)} %subtract_exponential_fusion.3, f32[4,896,896]{1,2,0:T(8,128)} %fusion.184, bf16[4,896,4,80]{1,3,2,0:T(8,128)(2,1)} %get-tuple-element.432), kind=kOutput, calls=%fused_computation.34.clone.1 | convolution fusion | flops 529863040 | bytes 53101568 | tf_op jit(solution)/shard_map/while/body/eval_jaxpr/gqk,qge->kge/dot_general | solution.py:73
  618.3 20.1 %fusion.185 = bf16[4,896,4,80]{1,3,2,0:T(8,128)(2,1)} fusion(bf16[4,896,4,80]{1,3,2,0:T(8,128)(2,1)} %get-tuple-element.416, s32[]{:T(128)} %get-tuple-element.415, f32[4,896,896]{1,2,0:T(8,128)} %subtract_exponential_fusion.3, f32[4,896,896]{1,2,0:T(8,128)} %fusion.184, bf16[4,896,4,80]{1,3,2,0:T(8,128)(2,1)} %get-tuple-element.430), kind=kOutput, calls=%fused_computation.32.clone.1 | convolution fusion | flops 529863040 | bytes 53101568 | tf_op jit(solution)/shard_map/while/body/eval_jaxpr/gqk,kge->qge/dot_general | solution.py:72
  685.3 21.1 %fusion.185 = bf16[4,896,4,80]{1,3,2,0:T(8,128)(2,1)} fusion(bf16[4,896,4,80]{1,3,2,0:T(8,128)(2,1)} %get-tuple-element.416, s32[]{:T(128)} %get-tuple-element.415, f32[4,896,896]{1,2,0:T(8,128)} %subtract_exponential_fusion.3, f32[4,896,896]{1,2,0:T(8,128)} %fusion.184, bf16[4,896,4,80]{1,3,2,0:T(8,128)(2,1)} %get-tuple-element.430), kind=kOutput, calls=%fused_computation.32.clone.1 | convolution fusion | flops 529863040 | bytes 53101568 | tf_op jit(solution)/shard_map/while/body/eval_jaxpr/gqk,kge->qge/dot_general | solution.py:72
  752.1 20.0 %fusion.185 = bf16[4,896,4,80]{1,3,2,0:T(8,128)(2,1)} fusion(bf16[4,896,4,80]{1,3,2,0:T(8,128)(2,1)} %get-tuple-element.416, s32[]{:T(128)} %get-tuple-element.415, f32[4,896,896]{1,2,0:T(8,128)} %subtract_exponential_fusion.3, f32[4,896,896]{1,2,0:T(8,128)} %fusion.184, bf16[4,896,4,80]{1,3,2,0:T(8,128)(2,1)} %get-tuple-element.430), kind=kOutput, calls=%fused_computation.32.clone.1 | convolution fusion | flops 529863040 | bytes 53101568 | tf_op jit(solution)/shard_map/while/body/eval_jaxpr/gqk,kge->qge/dot_general | solution.py:72
  798.0 19.9 %fusion.186 = bf16[4,896,4,80]{1,3,2,0:T(8,128)(2,1)} fusion(bf16[4,896,4,80]{1,3,2,0:T(8,128)(2,1)} %get-tuple-element.417, s32[]{:T(128)} %get-tuple-element.415, f32[4,896,896]{1,2,0:T(8,128)} %subtract_exponential_fusion.3, f32[4,896,896]{1,2,0:T(8,128)} %fusion.184, bf16[4,896,4,80]{1,3,2,0:T(8,128)(2,1)} %get-tuple-element.432), kind=kOutput, calls=%fused_computation.34.clone.1 | convolution fusion | flops 529863040 | bytes 53101568 | tf_op jit(solution)/shard_map/while/body/eval_jaxpr/gqk,qge->kge/dot_general | solution.py:73
  817.9 19.9 %fusion.185 = bf16[4,896,4,80]{1,3,2,0:T(8,128)(2,1)} fusion(bf16[4,896,4,80]{1,3,2,0:T(8,128)(2,1)} %get-tuple-element.416, s32[]{:T(128)} %get-tuple-element.415, f32[4,896,896]{1,2,0:T(8,128)} %subtract_exponential_fusion.3, f32[4,896,896]{1,2,0:T(8,128)} %fusion.184, bf16[4,896,4,80]{1,3,2,0:T(8,128)(2,1)} %get-tuple-element.430), kind=kOutput, calls=%fused_computation.32.clone.1 | convolution fusion | flops 529863040 | bytes 53101568 | tf_op jit(solution)/shard_map/while/body/eval_jaxpr/gqk,kge->qge/dot_general | solution.py:72
  870.6 28.4 %reduce-scatter.13.cloned.1.call-done = bf16[320,1280]{1,0:T(8,128)(2,1)} async-done(((bf16[1280,1280]{1,0:T(8,128)(2,1)}), bf16[320,1280]{1,0:T(8,128)(2,1)}) %reduce-scatter.13.cloned.1.call-update) | async-done | bytes 819216 | tf_op jit(solution)/shard_map/reduce_scatter | solution.py:267
  899.0 48.0 %reduce-scatter.17.cloned.1.call-done = bf16[320,1280]{1,0:T(8,128)(2,1)} async-done(((bf16[1280,1280]{1,0:T(8,128)(2,1)}), bf16[320,1280]{1,0:T(8,128)(2,1)}) %reduce-scatter.17.cloned.1.call-update) | async-done | bytes 819216 | tf_op jit(solution)/shard_map/reduce_scatter | solution.py:270
  947.2 47.9 %reduce-scatter.21.cloned.1.call-done = bf16[320,1280]{1,0:T(8,128)(2,1)} async-done(((bf16[1280,1280]{1,0:T(8,128)(2,1)}), bf16[320,1280]{1,0:T(8,128)(2,1)}) %reduce-scatter.21.cloned.1.call-update) | async-done | bytes 819216 | tf_op jit(solution)/shard_map/reduce_scatter | solution.py:273
  1002.0 41.1 %pmax.7 = f32[16]{0:T(128)S(1)} all-reduce(f32[16]{0:T(128)S(1)} %reduce_max.24), channel_id=1, replica_groups=mesh['fsdp'=4,'rep'=8] {'fsdp','rep'}, use_global_device_ids=true, to_apply=%region_55.56 | all-reduce | flops 16 | bytes 128 | tf_op jit(solution)/shard_map/pmax | solution.py:174
  1102.3 26.0 %all-reduce.36 = (bf16[320]{0:T(512)(128)(2,1)S(1)}, bf16[320]{0:T(512)(128)(2,1)S(1)}, bf16[320]{0:T(512)(128)(2,1)S(1)}, bf16[1280]{0:T(1024)(128)(2,1)S(1)}, ...) all-reduce(bf16[320]{0:T(512)(128)(2,1)S(1)} %dynamic-slice.24, ...), channel_id=15, replica_groups=mesh['fsdp'=4,'rep'=8] {'rep'}, use_global_device_ids=true, to_apply=%region_30.31.clone | all-reduce | flops 3840 | bytes 15360
  1130.9 26.0 %all-reduce.35 = (bf16[320]{0:T(512)(128)(2,1)S(1)}, bf16[320]{0:T(512)(128)(2,1)S(1)}, bf16[320]{0:T(512)(128)(2,1)S(1)}, bf16[1280]{0:T(1024)(128)(2,1)S(1)}, ...) all-reduce(bf16[320]{0:T(512)(128)(2,1)S(1)} %dynamic-update-slice., ...), channel_id=1, replica_groups=mesh['fsdp'=4,'rep'=8] {'rep'}, use_global_device_ids=true, to_apply=%add.8 | all-reduce | flops 3840 | bytes 15360
  1269.9 33.1 %all-gather.24.cloned.1.call-done = bf16[1280,1280]{1,0:T(8,128)(2,1)} async-done(((bf16[160,1280]{1,0:T(8,128)(2,1)}), bf16[1280,1280]{1,0:T(8,128)(2,1)}) %all-gather.24.cloned.1.call-update) | async-done | bytes 3276816 | tf_op jit(solution)/shard_map/all_gather | solution.py:376
  (395 shorter events, 542.9 us)
Async XLA Ops:
  7.2 50.9 %all-gather.10.cloned.1.call-start = ((), (), s32[]{:S(2)}) async-start(), calls=%async_computation.12 | async-start | bytes 4096000 | tf_op jit(solution)/shard_map/all_gather | solution.py:111
  8.1 97.0 %all-gather.12.cloned.1.call-start = ((), (), s32[]{:S(2)}) async-start(), calls=%async_computation.13 | async-start | bytes 4096000 | tf_op jit(solution)/shard_map/all_gather | solution.py:109
  8.8 143.2 %all-gather.14.cloned.1.call-start = ((), (), s32[]{:S(2)}) async-start(), calls=%async_computation.14 | async-start | bytes 4096000 | tf_op jit(solution)/shard_map/all_gather | solution.py:110
  9.5 222.0 %all-gather.16.cloned.1.call-start = ((), (), s32[]{:S(2)}) async-start(), calls=%async_computation.15 | async-start | bytes 4096000 | tf_op jit(solution)/shard_map/all_gather | solution.py:112
  10.1 317.3 %all-gather.18.cloned.1.call-start = ((), (), s32[]{:S(2)}) async-start(), calls=%async_computation.16 | async-start | bytes 16384000 | tf_op jit(solution)/shard_map/all_gather | solution.py:113
  10.7 445.3 %all-gather.20.cloned.1.call-start = ((), (), s32[]{:S(2)}) async-start(), calls=%async_computation.17 | async-start | bytes 16384000 | tf_op jit(solution)/shard_map/all_gather | solution.py:114
  11.3 857.2 %reduce-scatter.29.cloned.1.call-start = ((), (), s32[]{:S(2)}) async-start(), calls=%async_computation.26 | async-start | bytes 16384000 | tf_op jit(solution)/shard_map/reduce_scatter | solution.py:279
  505.3 364.1 %reduce-scatter.33.cloned.1.call-start = ((), (), s32[]{:S(2)}) async-start(), calls=%async_computation.29 | async-start | bytes 16384000 | tf_op jit(solution)/shard_map/reduce_scatter | solution.py:282
  525.7 344.4 %reduce-scatter.25.cloned.1.call-start = ((), (), s32[]{:S(2)}) async-start(), calls=%async_computation.24 | async-start | bytes 4096000 | tf_op jit(solution)/shard_map/reduce_scatter | solution.py:276
  575.1 323.9 %reduce-scatter.13.cloned.1.call-start = ((), (), s32[]{:S(2)}) async-start(), calls=%async_computation.18 | async-start | bytes 4096000 | tf_op jit(solution)/shard_map/reduce_scatter | solution.py:267
  580.2 265.4 %copy-start.20 = (f32[1280]{0:T(1024)S(1)}, f32[1280]{0:T(1024)}, u32[]{:S(2)}) copy-start(f32[1280]{0:T(1024)} %copy-done.19) | copy-start | bytes 15364
  580.2 265.4 %copy-start.22 = (f32[896]{0:T(1024)S(1)}, f32[896]{0:T(1024)}, u32[]{:S(2)}) copy-start(f32[896]{0:T(1024)} %copy-done.21) | copy-start | bytes 10756
  580.2 265.4 %copy-start.28 = (f32[896]{0:T(1024)S(1)}, f32[896]{0:T(1024)}, u32[]{:S(2)}) copy-start(f32[896]{0:T(1024)} %copy-done.27) | copy-start | bytes 10756
  580.2 265.4 %copy-start.36 = (f32[1280]{0:T(1024)S(1)}, f32[1280]{0:T(1024)}, u32[]{:S(2)}) copy-start(f32[1280]{0:T(1024)} %copy-done.35) | copy-start | bytes 15364
  853.3 93.7 %reduce-scatter.17.cloned.1.call-start = ((), (), s32[]{:S(2)}) async-start(), calls=%async_computation.20 | async-start | bytes 4096000 | tf_op jit(solution)/shard_map/reduce_scatter | solution.py:270
  860.9 134.2 %reduce-scatter.21.cloned.1.call-start = ((), (), s32[]{:S(2)}) async-start(), calls=%async_computation.22 | async-start | bytes 4096000 | tf_op jit(solution)/shard_map/reduce_scatter | solution.py:273
  868.4 185.9 %reduce-scatter.31.cloned.1.call-start = ((), (), s32[]{:S(2)}) async-start(), calls=%async_computation.27 | async-start | bytes 3686400 | tf_op jit(solution)/shard_map/reduce_scatter | solution.py:326
  869.4 212.9 %reduce-scatter.35.cloned.1.call-start = ((), (), s32[]{:S(2)}) async-start(), calls=%async_computation.30 | async-start | bytes 3686400 | tf_op jit(solution)/shard_map/reduce_scatter | solution.py:329
  870.0 311.9 %reduce-scatter.27.cloned.1.call-start = ((), (), s32[]{:S(2)}) async-start(), calls=%async_computation.25 | async-start | bytes 921600 | tf_op jit(solution)/shard_map/reduce_scatter | solution.py:323
  870.5 328.8 %reduce-scatter.15.cloned.1.call-start = ((), (), s32[]{:S(2)}) async-start(), calls=%async_computation.19 | async-start | bytes 921600 | tf_op jit(solution)/shard_map/reduce_scatter | solution.py:314
  899.0 319.5 %reduce-scatter.19.cloned.1.call-start = ((), (), s32[]{:S(2)}) async-start(), calls=%async_computation.21 | async-start | bytes 921600 | tf_op jit(solution)/shard_map/reduce_scatter | solution.py:317
  947.1 291.6 %reduce-scatter.23.cloned.1.call-start = ((), (), s32[]{:S(2)}) async-start(), calls=%async_computation.23 | async-start | bytes 921600 | tf_op jit(solution)/shard_map/reduce_scatter | solution.py:320
  995.1 269.3 %all-gather.22.cloned.1.call-start = ((), (), s32[]{:S(2)}) async-start(), calls=%async_computation.28 | async-start | bytes 3686400 | tf_op jit(solution)/shard_map/all_gather | solution.py:373
  1054.3 248.7 %all-gather.24.cloned.1.call-start = ((), (), s32[]{:S(2)}) async-start(), calls=%async_computation.31 | async-start | bytes 3686400 | tf_op jit(solution)/shard_map/all_gather | solution.py:376
  (76 other events, 4652.2 us)
Sparse Core Ops, SparseCore 0:
  9.9 48.1 all-gather.9
  59.9 45.0 all-gather.11
  106.9 45.0 all-gather.13
  153.7 45.0 all-gather.15
  200.5 126.8 all-gather.17
  329.1 126.8 all-gather.19
  505.4 124.9 reduce-scatter.28
  633.6 124.9 reduce-scatter.32
  761.6 45.0 reduce-scatter.24
  853.5 45.4 reduce-scatter.12
  902.0 45.0 reduce-scatter.16
  950.0 45.0 reduce-scatter.20
  997.4 42.3 reduce-scatter.30
  1042.0 40.1 reduce-scatter.34
  1084.4 30.7 reduce-scatter.26
  1117.4 29.8 reduce-scatter.14
  1149.4 29.9 reduce-scatter.18
  1181.6 31.7 reduce-scatter.22
  1215.1 49.2 all-gather.21
  1265.9 37.0 all-gather.23
where the time goes:
time: 1320 us
  matrix products  548 us (42%)
  waiting for transfers between devices  406 us (31%)
  blocking collectives  209 us (16%)
  other arithmetic  77.1 us (6%)
  local copies, waits for them, and re-layouts  52 us (4%)
  between operations  21 us (2%)
    unnamed x4, blocking collectives  87.8 us
    all_gather x1, waiting for transfers between devices, per_device(): lax.all_gather(w_up, 'fsdp', axis=0, tiled=True)  86.1 us
    dot_general x4, matrix products, attend_backward(): jnp.einsum('gqk,kge->qge', grad_raw, key_block, preferred_element_type=jn...  81.1 us
    dot_general x4, matrix products, attend_backward(): jnp.einsum('gqk,qge->kge', grad_raw, query_block, preferred_element_type=...  79.5 us
    all_gather x1, waiting for transfers between devices, per_device(): lax.all_gather(w_down, 'fsdp', axis=0, tiled=True)  68.5 us
    dot_general x1, matrix products, per_device(): jnp.dot(ffn_low, up_full, preferred_element_type=jnp.float32)  60.1 us
    dot_general x8, matrix products, block_scores(): jnp.einsum('qge,kge->gqk', query_block, key_block, preferred_element_type...  53.1 us
    reduce_scatter x1, waiting for transfers between devices, per_device(): lax.psum_scatter(grad_w_key.astype(jnp.bfloat16), 'fsdp', scatter_dimensi...  48 us
  transfers between devices with their start and end apart: 20, of which 11 were waited for; matrix products, arithmetic and copies ran while one was open for 46% of the time, Pallas kernels for 0%

commit v1 on v0

v1 whole, which is shorter than its diff:
```python
import functools

import jax
import jax.numpy as jnp
from jax import lax
from jax.experimental import pallas as pl
from jax.experimental.pallas import tpu as pltpu
from jax.sharding import PartitionSpec as P

H = 16
HD = 80
EPS = 1e-05
UNIT = 16.0
SCALE = HD ** (-0.5)
LOG2E = 1.4426950408889634
F32 = jnp.float32
BF = jnp.bfloat16
AXES = ("fsdp", "rep")
MIB = 1024 * 1024
VMEM = dict(
    unpack_vectors=8,
    pack_vectors=8,
    merge=4,
    pick=8,
    land=2,
    combine=16,
    assemble=20,
    norm_attn=8,
    project=20,
    attend=28,
    attend_back=36,
    out_project=44,
    up_project=32,
    down_back=44,
    down_project=44,
    up_back=52,
    out_back=24,
    input_back=44,
    wgrad_down=32,
    wgrad_up=40,
    wgrad_out=24,
    wgrad_qkv=44,
)


def dg(a, b, ca, cb):
    return lax.dot_general(a, b, (((ca,), (cb,)), ((), ())), preferred_element_type=F32)


class Clock:
    def __init__(self, on):
        self.on, self.deps, self.last, self.soon = on, [], [], []

    def wait(self, *values):
        self.deps += values

    def after_next(self, v):
        self.soon.append(v)
        return v

    def take(self):
        deps = self.deps + self.last if self.on else []
        self.deps, self.soon = self.soon, []
        return deps


CLOCK = [Clock(False)]


def pcall(kernel, *, out_shape, grid_spec=None, grid=None, in_specs=None, out_specs=None,
          deps=None, aliases=None, cost_estimate=None, name=None):
    spec = grid_spec or dict(grid=grid, in_specs=in_specs, out_specs=out_specs)
    npre = spec.get("num_scalar_prefetch", 0)
    nin = npre + len(spec["in_specs"])
    chained = deps is None
    deps = CLOCK[0].take() if chained else list(deps)
    spec = dict(spec, in_specs=list(spec["in_specs"]) + [ANY] * len(deps))
    spec["num_scalar_prefetch"] = npre

    def body(*refs):
        kernel(*refs[:nin], *refs[nin + len(deps) :])

    f = pl.pallas_call(
        body,
        grid_spec=pltpu.PrefetchScalarGridSpec(**spec),
        out_shape=out_shape,
        input_output_aliases=aliases or {},
        compiler_params=pltpu.CompilerParams(
            dimension_semantics=("arbitrary",) * len(spec["grid"]),
            vmem_limit_bytes=VMEM[name] * MIB,
        ),
        cost_estimate=cost_estimate,
        name=name,
    )

    def run(*args):
        out = f(*args, *deps)
        if chained:
            CLOCK[0].last = [jax.tree.leaves(out)[0]]
        return out

    return run


PACE = 1.0
COST = dict(wgrad_down=8, wgrad_up=9, wgrad_out=5, wgrad_qkv=9)


def cost(us):
    return pl.CostEstimate(
        flops=int(us * PACE * 1.15e9), bytes_accessed=1024, transcendentals=0
    )


def full(shape):
    return pl.BlockSpec(shape, lambda *_: (0,) * len(shape))


ANY = pl.BlockSpec(memory_space=pltpu.HBM)


class Weight:
    def __init__(self, chunks, width, rows, offs):
        self.chunks, self.width, self.rows, self.offs = chunks, width, rows, offs
        self.cols = width * len(chunks)
        self.total = None
        self.arrays = [a for arrays, _ in chunks for a in arrays]

    def copies(self, refs, offs, buf, sem, lo, hi, at=0):
        out = []
        k = len(self.rows)
        for c, (_, base) in enumerate(self.chunks):
            a, b = max(lo, c * self.width), min(hi, (c + 1) * self.width)
            if a >= b:
                continue
            for i in range(k):
                start = a - c * self.width + base[i]
                out.append(
                    pltpu.make_async_copy(
                        refs[c * k + i].at[:, pl.ds(start, b - a)],
                        buf.at[
                            pl.ds(pl.multiple_of(offs[i], 16), self.rows[i]),
                            pl.ds(at + a - lo, b - a),
                        ],
                        sem.at[len(out)],
                    )
                )
        return out


def start_all(copies):
    for c in copies:
        c.start()


def wait(copies):
    for c in copies:
        c.wait()


def stream(w, refs, offs, buf, sem, tile, j):
    nt = w.cols // tile

    def copies(i):
        return w.copies(refs, offs, buf.at[i % 2], sem.at[i % 2], i * tile, (i + 1) * tile)

    for i in range(nt):

        @pl.when(j == i)
        def _(i=i):
            if i == 0:
                start_all(copies(0))
            if i + 1 < nt:
                start_all(copies(i + 1))
            wait(copies(i))

    return lax.rem(j, 2)


def chunks_of(rows, step=128):
    return [(r, min(step, rows - r)) for r in range(0, rows, step)]


def groups_of(rows):
    first = 256
    second = (rows - first) // 256 * 128
    return [(0, first), (first, second), (first + second, rows - first - second)]


def absolute(f, items):
    a, b, c, d = items
    odd = f % 2 == 1
    a, b = jnp.where(odd, b, a), jnp.where(odd, a, b)
    c, d = jnp.where(odd, d, c), jnp.where(odd, c, d)
    high = f // 2 == 1
    return [
        jnp.where(high, c, a),
        jnp.where(high, d, b),
        jnp.where(high, a, c),
        jnp.where(high, b, d),
    ]


def unpack_vectors(shards, k, ku, f=None):
    n = len(shards)
    npre = 0 if f is None else 1

    def kernel(*rest):
        rows_ref, cols_ref, up_ref = rest[npre + n :]
        parts = [r[...].astype(F32) for r in rest[npre : npre + n]]
        if npre:
            parts = absolute(rest[0][0], parts)
        rows = [
            jnp.concatenate([p[:, i * k : (i + 1) * k] for p in parts], axis=1) for i in range(8)
        ]
        rows = jnp.concatenate(rows, axis=0)
        rows_ref[...] = rows
        cols_ref[...] = jnp.transpose(rows)
        up_ref[...] = jnp.concatenate([p[:, 8 * k : 8 * k + ku] for p in parts], axis=1)

    width = shards[0].shape[1]
    return pcall(
        kernel,
        grid_spec=dict(
            num_scalar_prefetch=npre,
            grid=(1,),
            in_specs=[full((1, width))] * n,
            out_specs=[full((8, n * k)), full((n * k, 8)), full((1, n * ku))],
        ),
        out_shape=[
            jax.ShapeDtypeStruct((8, n * k), F32),
            jax.ShapeDtypeStruct((n * k, 8), F32),
            jax.ShapeDtypeStruct((1, n * ku), F32),
        ],
            cost_estimate=cost(2),
        name="unpack_vectors",
    )(*([] if f is None else [f]), *shards)


def pack_vectors(f, n, first, sums_qkv, sums_ffn, sums_attn, grad_bd, grad_bu, stats):
    d = sums_ffn.shape[1]
    k, ku = d // n, grad_bu.shape[1] // n
    half = d // 2
    width = 8 * k + ku + 128

    def kernel(f_ref, first_ref, a_ref, b_ref, ffn_ref, attn_ref, bd_ref, bu_ref, st_ref, *outs):
        low = first_ref[0] == 0

        def row(i):
            a = jnp.transpose(a_ref[i])[0:1, :]
            b = jnp.transpose(b_ref[i])[0:1, :]
            return jnp.concatenate([jnp.where(low, a, b), jnp.where(low, b, a)], axis=1)

        rows = [
            row(0),
            row(1),
            ffn_ref[2:3, :],
            bd_ref[...],
            attn_ref[0:1, :],
            attn_ref[1:2, :],
            ffn_ref[0:1, :],
            ffn_ref[1:2, :],
        ]
        tops = jnp.max(st_ref[:, 1, :], axis=1, keepdims=True)
        tops = jnp.concatenate([jnp.broadcast_to(tops, (H, 128)), jnp.zeros((128 - H, 128), F32)])
        tops = jnp.transpose(tops)[0:1, :]
        owners = [
            jnp.concatenate(
                [r[:, i * k : (i + 1) * k] for r in rows]
                + [bu_ref[:, i * ku : (i + 1) * ku], tops],
                axis=1,
            )
            for i in range(n)
        ]
        if n == 4:
            owners = absolute(f_ref[0], owners)
        for o_ref, v in zip(outs, owners):
            o_ref[...] = v

    args = [*sums_qkv, sums_ffn, sums_attn, grad_bd, grad_bu, stats]
    return pcall(
        kernel,
        grid_spec=dict(
            num_scalar_prefetch=2,
            grid=(1,),
            in_specs=[full(a.shape) for a in args],
            out_specs=[full((1, width))] * n,
        ),
        out_shape=[jax.ShapeDtypeStruct((1, width), F32)] * n,
            cost_estimate=cost(2.7),
        name="pack_vectors",
    )(f, first, *args)


def norm_kernel(x_ref, v_ref, o_ref):
    v = x_ref[...].astype(F32)
    c = v - jnp.mean(v, axis=1, keepdims=True)
    r = lax.rsqrt(jnp.mean(c * c, axis=1, keepdims=True) + EPS)
    y = c * r * v_ref[4:5, :] + v_ref[5:6, :]
    o_ref[...] = jnp.transpose(y).astype(BF)


def norm_transposed(x, vrows):
    t, d = x.shape
    return pcall(
        norm_kernel,
        grid=(t // 128,),
        in_specs=[pl.BlockSpec((128, d), lambda i: (i, 0)), full((8, d))],
        out_specs=pl.BlockSpec((d, 128), lambda i: (0, i)),
        out_shape=jax.ShapeDtypeStruct((d, t), BF),
            cost_estimate=cost(6.7),
        name="norm_attn",
    )(x, vrows)


def project(w, xt, cols, col, tile=640):
    d, t = xt.shape
    n = w.cols
    k = len(w.arrays)

    def kernel(offs, x_ref, b_ref, *rest):
        refs = rest[:k]
        o_ref, buf, sem = rest[k:]
        slot = stream(w, refs, offs, buf, sem, tile, pl.program_id(0))
        out = dg(buf[slot], x_ref[...], 0, 0)
        if col is not None:
            out = out + b_ref[:, col : col + 1]
        o_ref[...] = out.astype(BF)

    return pcall(
        kernel,
        grid_spec=dict(
            num_scalar_prefetch=1,
            grid=(n // tile,),
            in_specs=[full((d, t)), pl.BlockSpec((tile, 8), lambda j, o: (j, 0))] + [ANY] * k,
            out_specs=pl.BlockSpec((tile, t), lambda j, o: (j, 0)),
            scratch_shapes=[pltpu.VMEM((2, d, tile), BF), pltpu.SemaphoreType.DMA((2, k))],
        ),
        out_shape=jax.ShapeDtypeStruct((n, t), BF),
            cost_estimate=cost(8.8),
        name="project",
    )(w.offs, xt, cols, *w.arrays)


HPG = 2


def attend_kernel(len_ref, q_ref, k_ref, v_ref, mixed_ref, stat_ref):
    t = q_ref.shape[1]
    row = lax.broadcasted_iota(jnp.int32, (16, t), 0)
    pos = lax.broadcasted_iota(jnp.int32, (16, t), 1)
    hidden = jnp.where((row == 0) & (pos >= len_ref[0]), -1e30, 0.0).astype(BF)
    ones = jnp.ones((16, t), BF)
    for g in range(HPG):
        rows = slice(g * HD, (g + 1) * HD)
        keys = jnp.concatenate([k_ref[rows, :], hidden], axis=0)
        queries = jnp.concatenate([q_ref[rows, :], ones], axis=0)
        values = jnp.concatenate([v_ref[rows, :], ones], axis=0)
        raw = dg(keys, queries, 0, 0)
        top = jnp.max(raw, axis=0, keepdims=True)
        expo = jnp.exp2((raw - top) * (SCALE * LOG2E)).astype(BF)
        out = dg(values, expo, 1, 0)
        total = out[HD : HD + 1, :]
        mixed_ref[rows, :] = (out[:HD, :] / total).astype(BF)
        stat_ref[g, 0:1, :] = top + jnp.log2(total) * (1.0 / (SCALE * LOG2E))
        stat_ref[g, 1:2, :] = top * SCALE
        stat_ref[g, 2:8, :] = jnp.zeros((6, t), F32)


def attend(valid, qt, kt, vt):
    d, t = qt.shape
    blk = pl.BlockSpec((HPG * HD, t), lambda i, o: (i, 0))
    return pcall(
        attend_kernel,
        grid_spec=dict(
            num_scalar_prefetch=1,
            grid=(H // HPG,),
            in_specs=[blk] * 3,
            out_specs=[blk, pl.BlockSpec((HPG, 8, t), lambda i, o: (i, 0, 0))],
        ),
        out_shape=[
            jax.ShapeDtypeStruct((d, t), BF),
            jax.ShapeDtypeStruct((H, 8, t), F32),
        ],
            cost_estimate=cost(21),
        name="attend",
    )(valid, qt, kt, vt)


def three_rows(v):
    hi = v.astype(BF).astype(F32)
    mid = (v - hi).astype(BF).astype(F32)
    low = (v - hi - mid).astype(BF).astype(F32)
    return [hi, mid, low]


def attend_back_kernel(
    len_ref, half_ref, q_ref, k_ref, v_ref, m_ref, dm_ref, stat_ref, o_ref, sum_ref
):
    t = q_ref.shape[1]
    row = lax.broadcasted_iota(jnp.int32, (16, t), 0)
    pos = lax.broadcasted_iota(jnp.int32, (16, t), 1)
    key_rows = jnp.where(
        row < 3, 1.0, jnp.where((row == 3) & (pos >= len_ref[0]), -1e30, 0.0)
    ).astype(BF)
    value_rows = jnp.where(row < 3, 1.0, 0.0).astype(BF)
    one = jnp.ones((1, t), F32)
    zeros = jnp.zeros((12, t), F32)
    for g in range(HPG):
        rows = slice(g * HD, (g + 1) * HD)
        qt, kt, vt, dm = q_ref[rows, :], k_ref[rows, :], v_ref[rows, :], dm_ref[rows, :]
        inner = jnp.sum(dm.astype(F32) * m_ref[rows, :].astype(F32), axis=0, keepdims=True)
        q_rows = jnp.concatenate(three_rows(-stat_ref[g, 0:1, :]) + [one, zeros], axis=0)
        d_rows = jnp.concatenate(three_rows(-inner) + [one, zeros], axis=0)
        shifted = dg(
            jnp.concatenate([qt, q_rows.astype(BF)], axis=0),
            jnp.concatenate([kt, key_rows], axis=0),
            0,
            0,
        )
        probs = jnp.exp2(shifted * (SCALE * LOG2E))
        grad_probs = dg(
            jnp.concatenate([dm, d_rows.astype(BF)], axis=0),
            jnp.concatenate([vt, value_rows], axis=0),
            0,
            0,
        )
        grad_scores = (probs * grad_probs).astype(BF)
        grad_v = dg(dm, probs.astype(BF), 1, 0).astype(BF)
        grad_k = (dg(qt, grad_scores, 1, 0) * SCALE).astype(BF)
        grad_q = (dg(kt, grad_scores, 1, 1) * SCALE).astype(BF)
        o_ref[0, rows, :] = grad_q
        o_ref[1, rows, :] = grad_k
        o_ref[2, rows, :] = grad_v
        for i, v in enumerate((grad_q, grad_v)):
            total = jnp.sum(v.astype(F32), axis=1, keepdims=True)
            sum_ref[i, rows, :] = jnp.broadcast_to(total, (HD, 8))


def attend_back(valid, half, qt, kt, vt, mixed, grad_mixed, stats):
    d, t = qt.shape
    steps = H // HPG // 2
    rows = HPG * HD
    blk = pl.BlockSpec((rows, t), lambda i, v, h: (h[0] * steps + i, 0))
    return pcall(
        attend_back_kernel,
        grid_spec=dict(
            num_scalar_prefetch=2,
            grid=(steps,),
            in_specs=[blk] * 5
            + [pl.BlockSpec((HPG, 8, t), lambda i, v, h: (h[0] * steps + i, 0, 0))],
            out_specs=[
                pl.BlockSpec((3, rows, t), lambda i, v, h: (0, i, 0)),
                pl.BlockSpec((2, rows, 8), lambda i, v, h: (0, i, 0)),
            ],
        ),
        out_shape=[
            jax.ShapeDtypeStruct((3, d // 2, t), BF),
            jax.ShapeDtypeStruct((2, d // 2, 8), F32),
        ],
            cost_estimate=cost(19),
        name="attend_back",
    )(valid, half, qt, kt, vt, mixed, grad_mixed, stats)


def out_project(w, mixed_t, frames, vrows, tile=640):
    d, t = mixed_t.shape
    k = len(w.arrays)
    nt = d // tile

    def kernel(offs, m_ref, x_ref, v_ref, *rest):
        refs = rest[:k]
        mid_ref, low_ref, lowt_ref, buf, sem = rest[k:]
        j = pl.program_id(0)
        slot = stream(w, refs, offs, buf, sem, tile, j)
        out = dg(m_ref[...], buf[slot], 0, 0)
        for s in range(nt):

            @pl.when(j == s)
            def _():
                cols = slice(s * tile, (s + 1) * tile)
                mid_ref[:, cols] = out + x_ref[:, cols].astype(F32) + v_ref[2:3, cols]

        @pl.when(j == nt - 1)
        def _():
            for i in range(t // 128):
                rows = slice(i * 128, (i + 1) * 128)
                v = mid_ref[rows, :]
                c = v - jnp.mean(v, axis=1, keepdims=True)
                r = lax.rsqrt(jnp.mean(c * c, axis=1, keepdims=True) + EPS)
                y = c * r * v_ref[6:7, :] + v_ref[7:8, :]
                low_ref[rows, :] = y.astype(BF)
                lowt_ref[:, rows] = jnp.transpose(y).astype(BF)

    return pcall(
        kernel,
        grid_spec=dict(
            num_scalar_prefetch=1,
            grid=(nt,),
            in_specs=[full((d, t)), full((t, d)), full((8, d))] + [ANY] * k,
            out_specs=[full((t, d)), full((t, d)), full((d, t))],
            scratch_shapes=[pltpu.VMEM((2, d, tile), BF), pltpu.SemaphoreType.DMA((2, k))],
        ),
        out_shape=[
            jax.ShapeDtypeStruct((t, d), F32),
            jax.ShapeDtypeStruct((t, d), BF),
            jax.ShapeDtypeStruct((d, t), BF),
        ],
            cost_estimate=cost(15),
        name="out_project",
    )(w.offs, mixed_t, frames, vrows, *w.arrays)


def gelu_pair(v):
    d = jnp.abs(v) * (0.3275911 * 0.7071067811865476) + 1.0
    k = pl.reciprocal(d, approx=True)
    k = k * (2.0 - d * k)
    e = jnp.exp2(v * v * (-0.5 * LOG2E))
    poly = k * (
        0.5 * 0.254829592
        + k
        * (
            0.5 * -0.284496736
            + k * (0.5 * 1.421413741 + k * (0.5 * -1.453152027 + k * (0.5 * 1.061405429)))
        )
    )
    tail = poly * e
    cdf = jnp.where(v >= 0, 1.0 - tail, tail)
    return v * cdf, cdf + v * e * 0.3989422804014327


def up_project(w, low, bias, tile=1280, sub=256):
    t, d = low.shape
    n = w.cols
    k = len(w.arrays)

    def kernel(offs, x_ref, b_ref, *rest):
        refs = rest[:k]
        h_ref, g_ref, buf, sem = rest[k:]
        slot = stream(w, refs, offs, buf, sem, tile, pl.program_id(0))
        for s in range(tile // sub):
            cols = slice(s * sub, (s + 1) * sub)
            for r, size in chunks_of(t):
                rows = slice(r, r + size)
                before = dg(x_ref[rows, :], buf[slot, :, cols], 1, 0) + b_ref[:, cols]
                hidden, slope = gelu_pair(before)
                h_ref[rows, cols] = hidden.astype(BF)
                g_ref[rows, cols] = slope.astype(BF)

    blk = pl.BlockSpec((t, tile), lambda j, o: (0, j))
    return pcall(
        kernel,
        grid_spec=dict(
            num_scalar_prefetch=1,
            grid=(n // tile,),
            in_specs=[full((t, d)), pl.BlockSpec((1, tile), lambda j, o: (0, j))] + [ANY] * k,
            out_specs=[blk, blk],
            scratch_shapes=[pltpu.VMEM((2, d, tile), BF), pltpu.SemaphoreType.DMA((2, k))],
        ),
        out_shape=[jax.ShapeDtypeStruct((t, n), BF)] * 2,
            cost_estimate=cost(32),
        name="up_project",
    )(w.offs, low, bias, *w.arrays)


def down_back(f, w, cot, slope, tile=1280):
    t, d = cot.shape
    n = slope.shape[1]
    k = len(w.arrays)
    nt = n // tile

    def kernel(offs, f_ref, c_ref, s_ref, *rest):
        refs = rest[:k]
        o_ref, b_ref, buf, sem = rest[k:]
        j = pl.program_id(0)
        copies = w.copies(refs, offs, buf, sem, 0, d)

        @pl.when(j == 0)
        def _():
            start_all(copies)
            wait(copies[:1])

        @pl.when(j == 1)
        def _():
            wait(copies[1:])

        rows = pl.ds(pl.multiple_of(j * tile, tile), tile)
        grad = dg(c_ref[...], buf[rows, :], 1, 1) * s_ref[...].astype(F32)
        low = grad.astype(BF)
        o_ref[...] = low
        b_ref[...] = jnp.sum(low.astype(F32), axis=0, keepdims=True)

    def place(j, o, f):
        return (0, jnp.bitwise_xor(j, f[0]))

    return pcall(
        kernel,
        grid_spec=dict(
            num_scalar_prefetch=2,
            grid=(nt,),
            in_specs=[full((t, d)), pl.BlockSpec((t, tile), place)] + [ANY] * k,
            out_specs=[pl.BlockSpec((t, tile), place), pl.BlockSpec((1, tile), place)],
            scratch_shapes=[pltpu.VMEM((n, d), BF), pltpu.SemaphoreType.DMA((k,))],
        ),
        out_shape=[jax.ShapeDtypeStruct((t, n), BF), jax.ShapeDtypeStruct((1, n), F32)],
            cost_estimate=cost(20),
        name="down_back",
    )(w.offs, f, cot, slope, *w.arrays)


def down_project(f, w, hidden, middle, vrows):
    t, d = middle.shape
    n = hidden.shape[1]
    k = len(w.arrays)
    nb = 4
    blk = n // nb

    def kernel(offs, f_ref, h_ref, m_ref, v_ref, *rest):
        refs = rest[:k]
        o_ref, wbuf, hbuf, mbuf, obuf, wsem, hsem, msem, osem = rest[k:]
        wc = w.copies(refs, offs, wbuf, wsem, 0, d)
        groups = groups_of(t)
        hc = []
        for g, (r, size) in enumerate(groups):
            hc.append([])
            for i in range(nb):
                owner = jnp.bitwise_xor(f_ref[0], i)
                cols = pl.ds(pl.multiple_of(owner * blk, blk), blk)
                here = pl.ds(r, size)
                hc[g].append(
                    pltpu.make_async_copy(
                        h_ref.at[here, cols],
                        hbuf.at[here, pl.ds(i * blk, blk)],
                        hsem.at[g, i],
                    )
                )
        mc = pltpu.make_async_copy(m_ref, mbuf, msem.at[0])
        start_all(hc[0] + wc + [mc] + hc[1] + hc[2])
        oc = []
        for i, (r, size) in enumerate(groups):
            rows = slice(r, r + size)
            wait(hc[i])
            if i == 0:
                wait(wc[:1])
                acc = dg(hbuf[rows, :blk], wbuf[:blk, :], 1, 0)
                wait(wc[1:])
                acc = acc + dg(hbuf[rows, blk:], wbuf[blk:, :], 1, 0)
                wait([mc])
            else:
                acc = dg(hbuf[rows, :], wbuf[...], 1, 0)
            obuf[rows, :] = (acc + mbuf[rows, :] + v_ref[3:4, :]).astype(BF)
            c = pltpu.make_async_copy(obuf.at[rows, :], o_ref.at[rows, :], osem.at[i])
            c.start()
            oc.append(c)
        wait(oc)

    return pcall(
        kernel,
        grid_spec=dict(
            num_scalar_prefetch=2,
            grid=(1,),
            in_specs=[ANY, ANY, full((8, d))] + [ANY] * k,
            out_specs=ANY,
            scratch_shapes=[
                pltpu.VMEM((n, d), BF),
                pltpu.VMEM((t, n), BF),
                pltpu.VMEM((t, d), F32),
                pltpu.VMEM((t, d), BF),
                pltpu.SemaphoreType.DMA((k,)),
                pltpu.SemaphoreType.DMA((3, nb)),
                pltpu.SemaphoreType.DMA((1,)),
                pltpu.SemaphoreType.DMA((8,)),
            ],
        ),
        out_shape=jax.ShapeDtypeStruct((t, d), BF),
            cost_estimate=cost(23),
        name="down_project",
    )(w.offs, f, hidden, middle, vrows, *w.arrays)


def norm_back(v, e, gain):
    c = v - jnp.mean(v, axis=1, keepdims=True)
    r = lax.rsqrt(jnp.mean(c * c, axis=1, keepdims=True) + EPS)
    xhat = c * r
    eg = e * gain
    grad = r * (
        eg
        - jnp.mean(eg, axis=1, keepdims=True)
        - xhat * jnp.mean(eg * xhat, axis=1, keepdims=True)
    )
    return grad, e * xhat


def up_back(w, grad_before, middle, cot, vrows, parts=4):
    t, d = cot.shape
    n = w.cols
    k = len(w.arrays)
    kk = len(w.rows)
    blk = n // parts

    def kernel(offs, gb_ref, m_ref, c_ref, v_ref, *rest):
        refs = rest[:k]
        gm_ref, low_ref, sums_ref = rest[k : k + 3]
        wbuf, gbuf, mbuf, cbuf, obuf, lbuf, wsem, gsem, osem = rest[k + 3 :]
        groups = groups_of(t)
        wc = [
            w.copies(refs, offs, wbuf, wsem.at[i], i * blk, (i + 1) * blk, i * blk)
            for i in range(parts)
        ]

        def rows_of(src, dst, sem):
            return [
                pltpu.make_async_copy(src.at[pl.ds(r, size)], dst.at[pl.ds(r, size)], sem.at[i])
                for i, (r, size) in enumerate(groups)
            ]

        gc, mc, cc = (
            rows_of(*v)
            for v in (
                (gb_ref, gbuf, gsem.at[0]),
                (m_ref, mbuf, gsem.at[1]),
                (c_ref, cbuf, gsem.at[2]),
            )
        )
        start_all(gc[:1])
        for c in wc:
            start_all(c)
        start_all([mc[0], cc[0], gc[1], mc[1], cc[1], gc[2], mc[2], cc[2]])
        oc = []
        sums = [jnp.zeros((1, d), F32)] * 3
        for i, (r, size) in enumerate(groups):
            wait([gc[i]])
            if i == 0:
                e = None
                for p in range(parts):
                    wait(wc[p])
                    cols = slice(p * blk, (p + 1) * blk)
                    part = dg(gbuf[r : r + size, cols], wbuf[:, cols], 1, 1)
                    e = part if e is None else e + part
            else:
                e = dg(gbuf[r : r + size, :], wbuf[...], 1, 1)
            wait([mc[i], cc[i]])
            for q, n128 in chunks_of(size):
                rows = slice(r + q, r + q + n128)
                eq = e[q : q + n128]
                grad, ex = norm_back(mbuf[rows, :], eq, v_ref[6:7, :])
                gm = cbuf[rows, :].astype(F32) + grad
                low = gm.astype(BF)
                obuf[rows, :] = gm
                lbuf[rows, :] = low
                terms = (ex, eq, low.astype(F32))
                sums = [a + jnp.sum(b, axis=0, keepdims=True) for a, b in zip(sums, terms)]
                out = [
                    pltpu.make_async_copy(
                        obuf.at[rows, :], gm_ref.at[rows, :], osem.at[0, len(oc)]
                    ),
                    pltpu.make_async_copy(
                        lbuf.at[rows, :], low_ref.at[rows, :], osem.at[1, len(oc)]
                    ),
                ]
                start_all(out)
                oc.append(out)
        sums_ref[...] = jnp.concatenate(sums + [jnp.zeros((5, d), F32)], axis=0)
        for c in oc:
            wait(c)

    return pcall(
        kernel,
        grid_spec=dict(
            num_scalar_prefetch=1,
            grid=(1,),
            in_specs=[ANY, ANY, ANY, full((8, d))] + [ANY] * k,
            out_specs=[ANY, ANY, full((8, d))],
            scratch_shapes=[
                pltpu.VMEM((d, n), BF),
                pltpu.VMEM((t, n), BF),
                pltpu.VMEM((t, d), F32),
                pltpu.VMEM((t, d), BF),
                pltpu.VMEM((t, d), F32),
                pltpu.VMEM((t, d), BF),
                pltpu.SemaphoreType.DMA((parts, kk)),
                pltpu.SemaphoreType.DMA((3, 3)),
                pltpu.SemaphoreType.DMA((2, 8)),
            ],
        ),
        out_shape=[
            jax.ShapeDtypeStruct((t, d), F32),
            jax.ShapeDtypeStruct((t, d), BF),
            jax.ShapeDtypeStruct((8, d), F32),
        ],
            cost_estimate=cost(28),
        name="up_back",
    )(w.offs, grad_before, middle, cot, vrows, *w.arrays)


def out_back(w, grad_attn):
    t, d = grad_attn.shape
    k = len(w.arrays)

    def kernel(offs, ga_ref, *rest):
        refs = rest[:k]
        o_ref, buf, sem = rest[k:]
        copies = w.copies(refs, offs, buf, sem, 0, w.cols)
        start_all(copies)
        wait(copies)
        o_ref[...] = dg(buf[...], ga_ref[...], 1, 1).astype(BF)

    return pcall(
        kernel,
        grid_spec=dict(
            num_scalar_prefetch=1,
            grid=(1,),
            in_specs=[full((t, d))] + [ANY] * k,
            out_specs=full((d, t)),
            scratch_shapes=[pltpu.VMEM((d, w.cols), BF), pltpu.SemaphoreType.DMA((k,))],
        ),
        out_shape=jax.ShapeDtypeStruct((d, t), BF),
            cost_estimate=cost(9),
        name="out_back",
    )(w.offs, grad_attn, *w.arrays)


def input_back(first, ws, halves, grad_middle, frames, vrows):
    d = 2 * halves[0].shape[1]
    t = halves[0].shape[2]
    k = len(ws[0].arrays)

    def kernel(offs, first_ref, a_ref, b_ref, gm_ref, x_ref, v_ref, *rest):
        refs = [rest[i * k : (i + 1) * k] for i in range(3)]
        o_ref, sums_ref = rest[3 * k : 3 * k + 2]
        wbuf, dbuf, gbuf, xbuf, obuf, wsem, dsem, msem, osem = rest[3 * k + 2 :]
        groups = groups_of(t)
        wc = [ws[i].copies(refs[i], offs, wbuf, wsem.at[i], 0, d, i * d) for i in range(3)]
        dc = []
        for g, (r, size) in enumerate(groups):
            dc.append([])
            for i in range(3):
                for h, ref in enumerate((a_ref, b_ref)):
                    spot = i * d + jnp.bitwise_xor(first_ref[0], h) * (d // 2)
                    dc[g].append(
                        pltpu.make_async_copy(
                            ref.at[i, :, pl.ds(r, size)],
                            dbuf.at[pl.ds(pl.multiple_of(spot, 128), d // 2), pl.ds(r, size)],
                            dsem.at[g, i, h],
                        )
                    )
        mc = [
            pltpu.make_async_copy(gm_ref, gbuf, msem.at[0]),
            pltpu.make_async_copy(x_ref, xbuf, msem.at[1]),
        ]
        start_all(dc[0])
        for c in wc:
            start_all(c)
        start_all(mc + dc[1] + dc[2])
        oc = []
        sums = [jnp.zeros((1, d), F32)] * 2
        for i, (r, size) in enumerate(groups):
            group = slice(r, r + size)
            wait(dc[i])
            if i == 0:
                e = None
                for p in range(3):
                    wait(wc[p])
                    ks = slice(p * d, (p + 1) * d)
                    part = dg(dbuf[ks, group], wbuf[:, ks], 0, 1)
                    e = part if e is None else e + part
                wait(mc)
            else:
                e = dg(dbuf[:, group], wbuf[...], 0, 1)
            for q, n128 in chunks_of(size):
                rows = slice(r + q, r + q + n128)
                eq = e[q : q + n128]
                grad, ex = norm_back(xbuf[rows, :].astype(F32), eq, v_ref[4:5, :])
                obuf[rows, :] = gbuf[rows, :] + grad
                sums = [a + jnp.sum(b, axis=0, keepdims=True) for a, b in zip(sums, (ex, eq))]
                c = pltpu.make_async_copy(obuf.at[rows, :], o_ref.at[rows, :], osem.at[len(oc)])
                c.start()
                oc.append(c)
        sums_ref[...] = jnp.concatenate(sums + [jnp.zeros((6, d), F32)], axis=0)
        wait(oc)

    return pcall(
        kernel,
        grid_spec=dict(
            num_scalar_prefetch=2,
            grid=(1,),
            in_specs=[ANY] * 4 + [full((8, d))] + [ANY] * (3 * k),
            out_specs=[ANY, full((8, d))],
            scratch_shapes=[
                pltpu.VMEM((d, 3 * d), BF),
                pltpu.VMEM((3 * d, t), BF),
                pltpu.VMEM((t, d), F32),
                pltpu.VMEM((t, d), BF),
                pltpu.VMEM((t, d), F32),
                pltpu.SemaphoreType.DMA((3, k)),
                pltpu.SemaphoreType.DMA((3, 3, 2)),
                pltpu.SemaphoreType.DMA((2,)),
                pltpu.SemaphoreType.DMA((8,)),
            ],
        ),
        out_shape=[jax.ShapeDtypeStruct((t, d), F32), jax.ShapeDtypeStruct((8, d), F32)],
            cost_estimate=cost(22),
        name="input_back",
    )(
        ws[0].offs,
        first,
        *halves,
        grad_middle,
        frames,
        vrows,
        *ws[0].arrays,
        *ws[1].arrays,
        *ws[2].arrays,
    )


def wgrad(name, order, side, left, right, mode, addends, groups, owners, sides=2):
    nb = order.shape[0]
    per = nb // groups
    down, heads = mode == "down", mode == "heads"
    if down:
        t, n = left.shape
        blk = n // owners // sides
        width = right.shape[1]
        grid, tile = nb, width
    else:
        d, t = left.shape
        blk = d // owners
        width = right.shape[0] * right.shape[1] if heads else right.shape[1] // 2
        tile = width if heads else min(width, 1280)
        grid = width // tile

    def kernel(order_ref, side_ref, *rest):
        if down:
            i = pl.program_id(0)
            part = dg(rest[0][...], rest[1][...], 0, 0)
            add, outs = rest[2 : 2 + len(addends)], rest[2 + len(addends) :]
            for g in range(groups):

                @pl.when((i >= g * per) & (i < (g + 1) * per))
                def _(g=g):
                    v = part
                    if add:
                        v = v + add[g][...].astype(F32)
                    outs[g][...] = v.astype(BF)

            return
        r_ref = rest[nb]
        add, outs = rest[nb + 1 : nb + 1 + len(addends)], rest[nb + 1 + len(addends) :]
        for g in range(groups):
            lhs = jnp.concatenate([r[...] for r in rest[g * per : (g + 1) * per]], axis=0)
            if heads:
                rhs = r_ref[...].reshape(tile, t)
                v = dg(lhs, rhs, 1, 1)
            else:
                v = dg(lhs, r_ref[...], 1, 0)
            if add:
                v = v + add[g][...].astype(F32)
            outs[g][...] = v.astype(BF)

    rows = per * blk
    if down:

        def out_spec(g):
            return pl.BlockSpec(
                (blk, width), lambda i, o, s: (jnp.clip(i - g * per, 0, per - 1), 0)
            )

        outs = [out_spec(g) for g in range(groups)]
        in_specs = [
            pl.BlockSpec((t, blk), lambda i, o, s: (0, sides * o[i] + s[0])),
            full((t, width)),
        ]
        args = [left, right]
    else:
        outs = [pl.BlockSpec((rows, tile), lambda j, o, s: (0, j))] * groups
        in_specs = [
            pl.BlockSpec((blk, t), functools.partial(lambda b, j, o, s: (o[b], 0), b))
            for b in range(nb)
        ]
        args = [left] * nb + [right]
        if heads:
            in_specs.append(full(right.shape))
        else:
            in_specs.append(pl.BlockSpec((t, tile), lambda j, o, s: (0, s[0] * grid + j)))
    k = right.shape[0] if down else t
    return pcall(
        kernel,
        grid_spec=dict(
            num_scalar_prefetch=2,
            grid=(grid,),
            in_specs=in_specs + outs[: len(addends)],
            out_specs=outs,
        ),
        out_shape=[jax.ShapeDtypeStruct((rows, width), BF)] * groups,
            cost_estimate=cost(COST[name]),
        name=name,
    )(order, side, *args, *addends)


def pick(v, start, rows, deps=None):
    width = v.shape[1]
    parts = 2 if rows % 32 == 0 else 1
    step = rows // parts

    def kernel(start_ref, v_ref, o_ref, buf, sem):
        ins, outs = [], []
        for i in range(parts):
            here = pl.ds(i * step, step)
            row = pl.ds(pl.multiple_of(start_ref[0] + i * step, 16), step)
            ins.append(pltpu.make_async_copy(v_ref.at[row], buf.at[here], sem.at[0, i]))
            outs.append(pltpu.make_async_copy(buf.at[here], o_ref.at[here], sem.at[1, i]))
        start_all(ins)
        for i in range(parts):
            ins[i].wait()
            outs[i].start()
        wait(outs)

    return pcall(
        kernel,
        grid_spec=dict(
            num_scalar_prefetch=1,
            grid=(1,),
            in_specs=[ANY],
            out_specs=ANY,
            scratch_shapes=[pltpu.VMEM((rows, width), v.dtype), pltpu.SemaphoreType.DMA((2, parts))],
        ),
        out_shape=jax.ShapeDtypeStruct((rows, width), v.dtype),
        deps=deps,
        cost_estimate=cost(1.8),
        name="pick",
    )(scalar(start), v)


def land(*values):
    out = pcall(
        lambda *refs: None,
        grid_spec=dict(grid=(1,), in_specs=[ANY] * len(values), out_specs=[ANY] * len(values)),
        out_shape=[jax.ShapeDtypeStruct(v.shape, v.dtype) for v in values],
        aliases={i: i for i in range(len(values))},
        cost_estimate=cost(0.3),
        name="land",
    )(*values)
    return out


def scalar(v):
    return jnp.asarray(v, jnp.int32).reshape(1)


class Relay:
    def __init__(self, net, shard):
        self.net, self.shard = net, shard
        self.rows = shard.shape[0] // 2

    def one(self, later=True):
        v = pick(self.shard, 0, 2 * self.rows) if later else self.shard
        self.s1 = self.net.move(v, "first")

    def one_done(self):
        net = self.net
        (self.s1,) = land(self.s1)
        self.t1 = net.move(self.s1, "core")
        self.s2 = net.move(pick(self.s1, net.c * self.rows, self.rows), "second")

    def two_done(self):
        (self.s2,) = land(self.s2)
        self.t2 = self.net.move(self.s2, "core")

    def weight(self, relative=False):
        net, r = self.net, self.rows
        ways = [0, 1 + net.c, 2 - net.c, 3, 3]
        parts = [0, 0, 0, net.c, 1 - net.c]
        owners = ways if relative else [net.f ^ w for w in ways]
        offs = offsets([o * (2 * r) + q * r for o, q in zip(owners, parts)])
        pieces = [self.shard, self.s1, self.t1, self.s2, self.t2]
        return Weight([(pieces, [0] * 5)], self.shard.shape[1], [2 * r] * 3 + [r] * 2, offs)


def offsets(values):
    return jnp.stack([jnp.asarray(v, jnp.int32) for v in values])


class Reduce:
    def __init__(self, net, make):
        self.net, self.make = net, make

    def theirs(self):
        net = self.net
        parts = self.make(net.order(1 - net.c), net.side(1 - net.c), [], 2)
        self.got = [net.move(p, "core") for p in parts]

    def mine(self):
        net = self.net
        send, self.kept = self.make(net.order(net.c), net.side(net.c), self.got, 2)
        self.p1 = net.move(send, "first")

    def second(self):
        rows = self.kept.shape[0] // 2
        on = combine([(self.kept, None, 1), (self.p1, None, 1)], rows)
        self.p2 = self.net.move(on, "second")


class Replicas:
    def __init__(self, net, r):
        self.net = net
        self.q = r.p2.shape[0] // 4
        self.terms = [r.kept, r.p1, r.p2]

    def own(self, block):
        return [(v, block, 0) for v in self.terms]

    def one(self):
        net = self.net
        v = combine(self.own(1 - net.zlow), 2 * self.q)
        self.r1 = net.move(v, "zlow")

    def two(self):
        net, q = self.net, self.q
        zl, zh = net.zlow, net.zhigh
        v = combine(self.own(2 * zl + 1 - zh) + [(self.r1, 1 - zh, 0)], q)
        self.r2 = net.move(v, "zhigh")

    def three(self):
        net, q = self.net, self.q
        zl, zh = net.zlow, net.zhigh
        self.mine = combine(self.own(2 * zl + zh) + [(self.r1, zh, 0), (self.r2, None, 0)], q)
        self.r3 = net.move(self.mine, "zhigh")
        self.r4 = net.move(self.mine, "zlow")

    def four(self):
        net = self.net
        (self.r3,) = land(self.r3)
        self.r5 = net.move(self.r3, "zlow")
        self.t = [net.move(v, "core") for v in (self.mine, self.r3)]

    def five(self):
        net = self.net
        self.r4, self.r5 = land(self.r4, self.r5)
        self.t += [net.move(v, "core") for v in (self.r4, self.r5)]

    def finish(self, widths, by_rows):
        net = self.net
        zl, zh = net.zlow, net.zhigh
        spots = [2 * zl + zh, 2 * zl + 1 - zh, 2 * (1 - zl) + zh, 2 * (1 - zl) + 1 - zh]
        pieces = [self.mine, self.r3, self.r4, self.r5] + self.t
        return assemble(pieces, offsets(spots + [net.c]), widths, by_rows)


def assemble(pieces, spots, widths, by_rows):
    q, w = pieces[0].shape
    starts = [sum(widths[:i]) for i in range(len(widths))]
    n = len(widths)

    def kernel(spot_ref, *rest):
        ins, outs = rest[:8], rest[8 : 8 + n]
        buf, wide, isem, osem = rest[8 + n :]
        loads = [pltpu.make_async_copy(ins[i], buf.at[i], isem.at[i]) for i in range(8)]
        start_all(loads)
        stores = []
        for i in range(8):
            side = spot_ref[4] if i < 4 else 1 - spot_ref[4]
            loads[i].wait()
            if i >= 2:
                wait(stores[i - 2])
            wide[i % 2] = buf[i].astype(F32)
            out = []
            for j in range(n):
                row = spot_ref[i % 4] * q
                if by_rows:
                    row = row + side * (4 * q)
                    cols = pl.ds(0, widths[j])
                else:
                    cols = pl.ds(pl.multiple_of(side * widths[j], 128), widths[j])
                out.append(
                    pltpu.make_async_copy(
                        wide.at[i % 2, :, pl.ds(starts[j], widths[j])],
                        outs[j].at[pl.ds(pl.multiple_of(row, 8), q), cols],
                        osem.at[i % 2, j],
                    )
                )
            start_all(out)
            stores.append(out)
        wait(stores[6] + stores[7])

    shapes = [(8 * q, v) if by_rows else (4 * q, 2 * v) for v in widths]
    return pcall(
        kernel,
        grid_spec=dict(
            num_scalar_prefetch=1,
            grid=(1,),
            in_specs=[ANY] * 8,
            out_specs=[ANY] * n,
            scratch_shapes=[
                pltpu.VMEM((8, q, w), BF),
                pltpu.VMEM((2, q, w), F32),
                pltpu.SemaphoreType.DMA((8,)),
                pltpu.SemaphoreType.DMA((2, n)),
            ],
        ),
        out_shape=[jax.ShapeDtypeStruct(v, F32) for v in shapes],
        cost_estimate=cost(5),
        name="assemble",
    )(spots, *pieces)


def combine(terms, rows):
    width = terms[0][0].shape[1]
    blk = rows
    while blk * width * 2 > 450 * 1024 and blk % 32 == 0:
        blk //= 2
    per = rows // blk
    moves = [scalar(0 if s is None else s) for _, s, _ in terms]

    def kernel(*refs):
        ins, o_ref = refs[len(terms) : -1], refs[-1]
        total = ins[0][...].astype(F32)
        for r in ins[1:]:
            total = total + r[...].astype(F32)
        o_ref[...] = total.astype(BF)

    def spec(i):
        fixed = terms[i][2] * per
        return pl.BlockSpec((blk, width), lambda j, *s: (s[i][0] * per + fixed + j, 0))

    return pcall(
        kernel,
        grid_spec=dict(
            num_scalar_prefetch=len(terms),
            grid=(per,),
            in_specs=[spec(i) for i in range(len(terms))],
            out_specs=pl.BlockSpec((blk, width), lambda j, *s: (j, 0)),
        ),
        out_shape=jax.ShapeDtypeStruct((rows, width), BF),
        cost_estimate=cost(3),
        name="combine",
    )(*moves, *[t[0] for t in terms])


class Net:
    def __init__(self, n, m):
        self.n, self.m = n, m
        self.f = lax.axis_index("fsdp")
        r = lax.axis_index("rep")
        self.c = r % 2
        self.zlow = (r // 2) % 2
        self.zhigh = r // 4

    def move(self, v, kind):
        pairs = []
        for f in range(self.n):
            for r in range(self.m):
                c = r % 2
                to_f, to_r = f, r
                if kind == "first":
                    to_f = f ^ (1 + c)
                elif kind == "second":
                    to_f = f ^ (2 - c)
                elif kind == "core":
                    to_r = r ^ 1
                elif kind == "zlow":
                    to_r = r ^ 2
                elif kind == "zhigh":
                    to_r = r ^ 4
                else:
                    to_f = f ^ kind
                pairs.append((f * self.m + r, to_f * self.m + to_r))
        out = lax.ppermute(v, AXES, pairs)
        return CLOCK[0].after_next(out) if kind == "core" else out

    def order(self, c):
        a, b = 1 + c, 2 - c
        return jnp.stack([self.f ^ a, self.f ^ 3, self.f, self.f ^ b]).astype(jnp.int32)

    def side(self, c):
        return jnp.asarray(c, jnp.int32)[None]


def merge(values, p):
    width = values[0].shape[1]

    def kernel(*refs):
        total = refs[0][...]
        lane = lax.broadcasted_iota(jnp.int32, (1, width), 1)
        for r in refs[1:-1]:
            v = r[...]
            total = jnp.where(lane < width - p, total + v, jnp.maximum(total, v))
        refs[-1][...] = total

    return pcall(
        kernel,
        grid_spec=dict(
            grid=(1,), in_specs=[full((1, width))] * len(values), out_specs=full((1, width))
        ),
        out_shape=jax.ShapeDtypeStruct((1, width), F32),
        cost_estimate=cost(1),
        name="merge",
    )(*values)


VECTOR_SPOTS = (0, 1, 2, 8, 3, 4, 5, 6, 7)


def finish(own, k, w_query, w_key, threshold, head_peak):
    gv = [own[i * k : (i + 1) * k] for i in range(8)] + [own[8 * k :]]
    limit = threshold[0].astype(F32) / UNIT
    factor = jnp.sqrt(limit / jnp.maximum(head_peak, limit))
    columns = jnp.broadcast_to(factor[:, None], (H, HD)).reshape(1, -1)
    clipped_query = (w_query.astype(F32) * columns).astype(BF)
    clipped_key = (w_key.astype(F32) * columns).astype(BF)
    return tuple(gv[i] for i in VECTOR_SPOTS) + (head_peak, factor, clipped_query, clipped_key)


def per_device(inputs, cotangent, lengths, threshold, *weights):
    n, m = lax.axis_size("fsdp"), lax.axis_size("rep")
    _, t, d = inputs.shape
    frames = inputs.reshape(t, d)
    cot = cotangent.reshape(t, d)
    index = lax.axis_index("fsdp") * m + lax.axis_index("rep")
    valid = lax.dynamic_slice_in_dim(lengths.reshape(-1), index, 1, 0)
    run = on_grid if (n, m) == (4, 8) else on_any
    layer_out, grad_inputs, matrices, vectors = run(
        n, m, frames, cot, valid, threshold, *weights
    )
    return (
        (layer_out.reshape(1, t, d), grad_inputs.reshape(1, t, d)) + tuple(matrices) + vectors
    )


def packed(vecs):
    return jnp.concatenate([vecs[VECTOR_SPOTS.index(i)] for i in range(9)])[None]


def on_grid(n, m, frames, cot, valid, threshold, wq_, wk_, wv_, wo_, wu_, wd_, *vecs):
    CLOCK[0] = clock = Clock(True)
    net = Net(n, m)
    t, d = frames.shape
    ff = wu_.shape[1]
    k = d // n
    h = d // 2
    f = scalar(net.f)
    gq, gk, gv, go, gu, gd = (Relay(net, w) for w in (wq_, wk_, wv_, wo_, wu_, wd_))

    gq.one(False)
    gk.one(False)
    shard = packed(vecs)
    v1, v2 = net.move(shard, "first"), net.move(shard, 3)
    gq.one_done()
    gv.one()
    v1, v2 = land(v1, v2)
    v3 = net.move(v1, "core")
    gk.one_done()
    vrows, vcols, bu = unpack_vectors(
        [shard, jnp.where(net.c == 0, v1, v3), jnp.where(net.c == 0, v3, v1), v2],
        k, ff // n, f,
    )
    normed_t = norm_transposed(frames, vrows)
    gq.two_done()
    clock.wait(gq.t2)
    qt = project(gq.weight(), normed_t, vcols, 0)
    gv.one_done()
    go.one()
    gk.two_done()
    clock.wait(gk.t2)
    kt = project(gk.weight(), normed_t, vcols, None)
    gv.two_done()
    clock.wait(gv.t2)
    vt = project(gv.weight(), normed_t, vcols, 1)
    go.one_done()
    gu.one()
    mixed, stats = attend(valid, qt, kt, vt)
    go.two_done()
    clock.wait(go.t2)
    middle, low, low_t = out_project(go.weight(), mixed, frames, vrows)
    gu.one_done()
    gd.one()
    gu.two_done()
    clock.wait(gu.t2)
    wu = gu.weight()
    hidden, slope = up_project(wu, low, bu)

    def maker(name, left, right, mode):
        def make(order, side, addends, groups):
            return wgrad(name, order, side, left, right, mode, addends, groups, n)

        return make

    rd = Reduce(net, maker("wgrad_down", hidden, cot, "down"))
    rd.theirs()
    gd.one_done()
    rd.mine()
    gd.two_done()
    clock.wait(gd.t2)
    wd = gd.weight(relative=True)
    grad_before, grad_bu = down_back(f, wd, cot, slope)
    ru = Reduce(net, maker("wgrad_up", low_t, grad_before, "cols"))
    ru.theirs()
    grad_middle, grad_attn, sums_ffn = up_back(wu, grad_before, middle, cot, vrows)
    rd.second()
    ru.mine()
    ro = Reduce(net, maker("wgrad_out", mixed, grad_attn, "cols"))
    ro.theirs()
    grad_mixed = out_back(go.weight(), grad_attn)
    ro.mine()
    zd = Replicas(net, rd)
    zd.one()
    theirs, own = net.side(1 - net.c), net.side(net.c)
    g_theirs, sums_theirs = attend_back(valid, theirs, qt, kt, vt, mixed, grad_mixed, stats)
    zd.two()
    halves = [g_theirs, None]

    def make_qkv(order, side, addends, groups):
        right = halves[1] if addends else halves[0]
        return wgrad("wgrad_qkv", order, side, normed_t, right, "heads", addends, groups, n)

    rq = Reduce(net, make_qkv)
    rq.theirs()
    ru.second()
    zd.three()
    halves[1], sums_own = attend_back(valid, own, qt, kt, vt, mixed, grad_mixed, stats)
    rq.mine()
    ro.second()
    zd.four()
    zu = Replicas(net, ru)
    zu.one()
    ws = [g.weight() for g in (gq, gk, gv)]
    grad_inputs, sums_attn = input_back(theirs, ws, halves, grad_middle, frames, vrows)
    rq.second()
    zu.two()
    zo = Replicas(net, ro)
    zo.one()
    zd.five()
    grad_bd = jnp.sum(cot.astype(F32), axis=0, keepdims=True)
    small = pack_vectors(
        f, n, theirs, (sums_theirs, sums_own), sums_ffn, sums_attn, grad_bd, grad_bu, stats
    )
    small = [small[0]] + [net.move(small[i], i) for i in (1, 2, 3)]
    layer_out = down_project(f, wd, hidden, middle, vrows)
    zq = Replicas(net, rq)
    zq.one()
    zu.three()
    zo.two()
    small = merge(small, 128)
    small = [small, net.move(small, "core")]
    (grad_w_down,) = zd.finish([d], True)
    zq.two()
    zo.three()
    zu.four()
    small = merge(small, 128)
    small = [small, net.move(small, "zlow")]
    zq.three()
    zo.four()
    zu.five()
    small = merge(small, 128)
    small = [small, net.move(small, "zhigh")]
    zo.five()
    (grad_w_up,) = zu.finish([ff // 2], False)
    zq.four()
    (grad_w_out,) = zo.finish([h], False)
    small = merge(small, 128)
    zq.five()
    qkv = zq.finish([h] * 3, False)
    vectors = finish(small[0, :-128], k, wq_, wk_, threshold, small[0, -128 : H - 128])
    return layer_out, grad_inputs, (*qkv, grad_w_out, grad_w_up, grad_w_down), vectors


def on_any(n, m, frames, cot, valid, threshold, wq_, wk_, wv_, wo_, wu_, wd_, *vecs):
    CLOCK[0] = Clock(False)
    t, d = frames.shape
    ff = wu_.shape[1]
    zero = jnp.zeros((1,), jnp.int32)
    order = jnp.arange(n, dtype=jnp.int32)

    def gather(shard):
        whole = lax.all_gather(shard, "fsdp", axis=0, tiled=True)
        return Weight([([whole], [0])], whole.shape[1], [whole.shape[0]], zero)

    def reduce(name, left, rights, mode):
        sides = []
        for i, right in enumerate(rights):
            (g,) = wgrad(name, order, zero + i, left, right, mode, [], 1, n, len(rights))
            g = lax.psum_scatter(g, "fsdp", scatter_dimension=0, tiled=True)
            sides.append(lax.psum(g, "rep"))
        return sides

    shard = packed(vecs)
    whole = lax.all_gather(shard, "fsdp", axis=0, tiled=True)
    shards = [whole[i : i + 1] for i in range(n)]
    vrows, vcols, bu = unpack_vectors(shards, d // n, ff // n)
    wq, wk, wv, wo, wu, wd = (gather(w) for w in (wq_, wk_, wv_, wo_, wu_, wd_))
    normed_t = norm_transposed(frames, vrows)
    qt = project(wq, normed_t, vcols, 0)
    kt = project(wk, normed_t, vcols, None)
    vt = project(wv, normed_t, vcols, 1)
    mixed, stats = attend(valid, qt, kt, vt)
    middle, low, low_t = out_project(wo, mixed, frames, vrows)
    hidden, slope = up_project(wu, low, bu)
    grad_before, grad_bu = down_back(zero, wd, cot, slope)
    grad_middle, grad_attn, sums_ffn = up_back(wu, grad_before, middle, cot, vrows)
    grad_mixed = out_back(wo, grad_attn)
    halves, sums = zip(
        *[
            attend_back(valid, zero + i, qt, kt, vt, mixed, grad_mixed, stats)
            for i in range(2)
        ]
    )
    grad_inputs, sums_attn = input_back(
        zero, (wq, wk, wv), halves, grad_middle, frames, vrows
    )
    layer_out = down_project(zero, wd, hidden, middle, vrows)
    down = reduce("wgrad_down", hidden, [cot], "down")
    up = reduce("wgrad_up", low_t, [grad_before] * 2, "cols")
    out = reduce("wgrad_out", mixed, [grad_attn] * 2, "cols")
    qkv = reduce("wgrad_qkv", normed_t, halves, "heads")
    h = d // 2
    matrices = [
        jnp.concatenate([s[:, i * h : (i + 1) * h] for s in qkv], axis=1).astype(F32)
        for i in range(3)
    ] + [
        jnp.concatenate(out, axis=1).astype(F32),
        jnp.concatenate(up, axis=1).astype(F32),
        down[0].astype(F32),
    ]
    grad_bd = jnp.sum(cot.astype(F32), axis=0, keepdims=True)
    rows = pack_vectors(
        zero, n, zero, sums, sums_ffn, sums_attn, grad_bd, grad_bu, stats
    )
    rows = jnp.concatenate(rows, axis=0)
    own = lax.psum_scatter(rows[:, :-128], "fsdp", scatter_dimension=0, tiled=True)
    own = lax.psum(own, "rep")[0]
    peaks = lax.pmax(rows[0, -128:], AXES)[:H]
    vectors = finish(own, d // n, wq_, wk_, threshold, peaks)
    return layer_out, grad_inputs, matrices, vectors


def solution(mesh):
    tokens = P(None, AXES, None)
    mat = P("fsdp", None)
    vec = P("fsdp")
    return jax.shard_map(
        per_device,
        mesh=mesh,
        in_specs=(tokens, tokens, P(), P()) + (mat,) * 6 + (vec,) * 9,
        out_specs=(tokens, tokens) + (mat,) * 6 + (vec,) * 9 + (P(), P(), mat, mat),
        check_vma=False,
    )
```

time: 1320 us -> 634 us (0.48)
  matrix products: 548 us -> 0 us
  Pallas kernels: 0 us -> 323 us
  waiting for transfers between devices: 406 us -> 151 us
  blocking collectives: 209 us -> 0 us
  other arithmetic: 77.1 us -> 2.58 us
  starting transfers between devices: 1.4 us -> 62.1 us
  local copies, waits for them, and re-layouts: 52 us -> 82.9 us
  between operations: 21 us -> 3.57 us
    dot_general x46 -> x0, matrix products: 548 us -> none  [the longest x4 81.1 us: attend_backward(): jnp.einsum('gqk,kge->qge', grad_raw, key_block, preferred_element_type=jn...]
    pallas_call x0 -> x79, Pallas kernels: none -> 323 us  [run(): out = f(*args, *deps)]
    all_gather x8 -> x0, waiting for transfers between devices: 276 us -> none  [the longest x1 86.1 us: per_device(): lax.all_gather(w_up, 'fsdp', axis=0, tiled=True)]
    ppermute x0 -> x85, waiting for transfers between devices: none -> 151 us  [move(): out = lax.ppermute(v, AXES, pairs)]
    reduce_scatter x12 -> x0, waiting for transfers between devices: 125 us -> none  [the longest x1 48 us: per_device(): lax.psum_scatter(grad_w_key.astype(jnp.bfloat16), 'fsdp', scatter_dimensi...]
    unnamed x4 -> x0, blocking collectives: 87.8 us -> none
    all_gather x5 -> x0, blocking collectives: 80.3 us -> none  [the longest x1 19.8 us: per_device(): lax.all_gather(shares[2].astype(jnp.bfloat16), 'rep', axis=0, tiled=True)]
    ppermute x0 -> x85, starting transfers between devices: none -> 62.1 us  [move(): out = lax.ppermute(v, AXES, pairs)]
  transfers between devices with their start and end apart: 20 -> 85, of which waited for: 11 -> 32; matrix products, arithmetic and copies ran while one was open for 46% -> 2% of each run, Pallas kernels for 0% -> 50%
where the time goes in v1:
time: 634 us; the launch traced here: 625 us
  Pallas kernels  323 us (51%)
  waiting for transfers between devices  151 us (24%)
  local copies, waits for them, and re-layouts  82.9 us (13%)
  starting transfers between devices  62.1 us (10%)
    pallas_call x79, Pallas kernels, run(): out = f(*args, *deps)  323 us
    ppermute x85, waiting for transfers between devices, move(): out = lax.ppermute(v, AXES, pairs)  151 us
    unnamed x304, local copies, waits for them, and re-layouts  74.2 us
    ppermute x85, starting transfers between devices, move(): out = lax.ppermute(v, AXES, pairs)  62.1 us
  transfers between devices with their start and end apart: 85, of which 32 were waited for; matrix products, arithmetic and copies ran while one was open for 2% of the time, Pallas kernels for 50%

profile of v1, /device:TPU:0, one launch (start us, length us, event | category | flops | bytes accessed | tf_op | source)
XLA Modules:
  0.0 624.8 jit_solution(3372565982039959066)
XLA Ops:
  3.7 10.5 %collective-permute-done.2.refs_0_ = bf16[320,1280]{1,0:T(8,128)(2,1)S(1)} collective-permute-done((bf16[320,1280]{1,0:T(8,128)(2,1)}, bf16[320,1280]{1,0:T(8,128)(2,1)S(1)}, u32[]{:S(2)}, u32[]{:S(2)}) %collective-permute-start.2) | collective-permute-done | bytes 819232 | tf_op jit(solution)/shard_map/ppermute | solution.py:1268
  85.8 20.0 %attend.1 = (bf16[1280,896]{1,0:T(8,128)(2,1)S(1)}, f32[16,8,896]{2,1,0:T(8,128)S(1)}) custom-call(s32[1]{0:T(128)} %bitcast.10.refs_0_, bf16[1280,896]{1,0:T(8,128)(2,1)S(1)} %copy-done.37, bf16[1280,896]{1,0:T(8,128)(2,1)S(1)} %project.4.refs_2_.refs_3_, bf16[1280,896]{1,0:T(8,128)(2,1)S(1)} %copy-done.41, bf16[320,5120]{1,0:T(8,128)(2,1)S(1)} %pick.16.refs_4_), custom_call_target="tpu_custom_call" | custom-call | flops 24149999616 | bytes 1024 | tf_op jit(solution)/shard_map/attend/pallas_call | solution.py:97
  111.3 12.1 %out_project.1 = (f32[896,1280]{1,0:T(8,128)}, bf16[896,1280]{1,0:T(8,128)(2,1)S(1)}, bf16[1280,896]{1,0:T(8,128)(2,1)S(1)}) custom-call(s32[5]{0:T(128)S(1)} %stack.50.refs_0_, bf16[1280,896]{1,0:T(8,128)(2,1)S(1)} %copy-done.45, bf16[896,1280]{1,0:T(8,128)(2,1)} %bitcast.39, f32[8,1280]{1,0:T(8,128)S(1)} %copy-done.140, bf16[320,1280]{1,0:T(8,128)(2,1)S(1)} %copy-done.81, ...), custom_call_target="tpu_custom_call" | custom-call | flops 17250000896 | bytes 1024 | tf_op jit(solution)/shard_map/out_project/pallas_call | solution.py:97
  136.1 15.4 %collective-permute-done.21.refs_0_ = bf16[160,5120]{1,0:T(8,128)(2,1)} collective-permute-done((bf16[160,5120]{1,0:T(8,128)(2,1)S(1)}, bf16[160,5120]{1,0:T(8,128)(2,1)}, u32[]{:S(2)}, u32[]{:S(2)}) %collective-permute-start.21) | collective-permute-done | bytes 1638432 | tf_op jit(solution)/shard_map/ppermute | solution.py:1268
  162.8 25.7 %up_project.1 = (bf16[896,5120]{1,0:T(8,128)(2,1)}, bf16[896,5120]{1,0:T(8,128)(2,1)}) custom-call(s32[5]{0:T(128)S(1)} %stack.50.refs_0_, bf16[896,1280]{1,0:T(8,128)(2,1)S(1)} %copy-done.142, f32[1,5120]{1,0:T(1,128)S(1)} %copy-done.148, bf16[320,5120]{1,0:T(8,128)(2,1)S(1)} %copy-done.20, bf16[320,5120]{1,0:T(8,128)(2,1)S(1)} %copy-done.4, ...), custom_call_target="tpu_custom_call" | custom-call | flops 36800000000 | bytes 1024 | tf_op jit(solution)/shard_map/up_project/pallas_call | solution.py:97
  192.1 11.6 %wgrad_down.2 = (bf16[1280,1280]{1,0:T(8,128)(2,1)}, bf16[1280,1280]{1,0:T(8,128)(2,1)}) custom-call(s32[4]{0:T(128)S(1)} %pad_add_fusion.refs_0_, s32[1]{0:T(128)} %bitcast.16.refs_1_, bf16[896,5120]{1,0:T(8,128)(2,1)S(1)} %copy-done.119, bf16[896,1280]{1,0:T(8,128)(2,1)S(1)} %bitcast.36, ...), custom_call_target="tpu_custom_call" | custom-call | flops 9200000000 | bytes 1024 | tf_op jit(solution)/shard_map/wgrad_down/pallas_call | solution.py:97
  209.9 9.4 %collective-permute-done.26.refs_3_.refs_5_ = bf16[1280,1280]{1,0:T(8,128)(2,1)} collective-permute-done((bf16[1280,1280]{1,0:T(8,128)(2,1)}, bf16[1280,1280]{1,0:T(8,128)(2,1)}, u32[]{:S(2)}, u32[]{:S(2)}) %collective-permute-start.26) | collective-permute-done | bytes 3276832 | tf_op jit(solution)/shard_map/ppermute | solution.py:1268
  221.2 11.7 %wgrad_down.3 = (bf16[1280,1280]{1,0:T(8,128)(2,1)S(1)}, bf16[1280,1280]{1,0:T(8,128)(2,1)S(1)}) custom-call(s32[4]{0:T(128)S(1)} %pad_add_fusion.1.refs_0_, s32[1]{0:T(128)} %bitcast.20.refs_1_, bf16[896,5120]{1,0:T(8,128)(2,1)} %get-tuple-element.83.refs_2_.refs_5_, bf16[896,1280]{1,0:T(8,128)(2,1)S(1)} %bitcast.37, ...), custom_call_target="tpu_custom_call" | custom-call | flops 9200000000 | bytes 1024 | tf_op jit(solution)/shard_map/wgrad_down/pallas_call | solution.py:97
  232.9 8.1 %collective-permute-done.27.refs_0_ = bf16[640,1280]{1,0:T(8,128)(2,1)} collective-permute-done((bf16[640,1280]{1,0:T(8,128)(2,1)S(1)}, bf16[640,1280]{1,0:T(8,128)(2,1)}, u32[]{:S(2)}, u32[]{:S(2)}) %collective-permute-start.27) | collective-permute-done | bytes 1638432 | tf_op jit(solution)/shard_map/ppermute | solution.py:1268
  248.5 17.9 %down_back.1 = (bf16[896,5120]{1,0:T(8,128)(2,1)}, f32[1,5120]{1,0:T(1,128)S(1)}) custom-call(s32[5]{0:T(128)S(1)} %stack.44.refs_0_, s32[1]{0:T(128)} %bitcast.4.refs_0_.refs_1_, bf16[896,1280]{1,0:T(8,128)(2,1)S(1)} %bitcast.38, bf16[896,5120]{1,0:T(8,128)(2,1)} %get-tuple-element.89.refs_3_, bf16[1280,1280]{1,0:T(8,128)(2,1)S(1)} %copy-done.14, ...), custom_call_target="tpu_custom_call" | custom-call | flops 23000000512 | bytes 1024 | tf_op jit(solution)/shard_map/down_back/pallas_call | solution.py:97
  266.4 11.0 %wgrad_up.2 = (bf16[640,2560]{1,0:T(8,128)(2,1)}, bf16[640,2560]{1,0:T(8,128)(2,1)}) custom-call(s32[4]{0:T(128)S(1)} %pad_add_fusion.refs_0_, s32[1]{0:T(128)} %bitcast.16.refs_1_, bf16[1280,896]{1,0:T(8,128)(2,1)S(1)} %copy-done.125, bf16[1280,896]{1,0:T(8,128)(2,1)S(1)} %copy-done.125, bf16[1280,896]{1,0:T(8,128)(2,1)S(1)} %copy-done.125, ...), custom_call_target="tpu_custom_call" | custom-call | flops 10350000128 | bytes 1024 | tf_op jit(solution)/shard_map/wgrad_up/pallas_call | solution.py:97
  278.0 26.4 %up_back.1 = (f32[896,1280]{1,0:T(8,128)}, bf16[896,1280]{1,0:T(8,128)(2,1)}, f32[8,1280]{1,0:T(8,128)S(1)}) custom-call(s32[5]{0:T(128)S(1)} %stack.50.refs_0_, bf16[896,5120]{1,0:T(8,128)(2,1)} %get-tuple-element.90.refs_6_.refs_8_.refs_1_, f32[896,1280]{1,0:T(8,128)} %get-tuple-element.82.refs_2_.refs_3_, bf16[896,1280]{1,0:T(8,128)(2,1)} %bitcast.35, ...), custom_call_target="tpu_custom_call" | custom-call | flops 32199999488 | bytes 1024 | tf_op jit(solution)/shard_map/up_back/pallas_call | solution.py:97
  312.1 11.2 %wgrad_up.3 = (bf16[640,2560]{1,0:T(8,128)(2,1)}, bf16[640,2560]{1,0:T(8,128)(2,1)S(1)}) custom-call(s32[4]{0:T(128)S(1)} %pad_add_fusion.1.refs_0_, s32[1]{0:T(128)} %bitcast.20.refs_1_, bf16[1280,896]{1,0:T(8,128)(2,1)S(1)} %copy-done.126, bf16[1280,896]{1,0:T(8,128)(2,1)S(1)} %copy-done.126, bf16[1280,896]{1,0:T(8,128)(2,1)S(1)} %copy-done.126, ...), custom_call_target="tpu_custom_call" | custom-call | flops 10350000128 | bytes 1024 | tf_op jit(solution)/shard_map/wgrad_up/pallas_call | solution.py:97
  342.1 17.2 %attend_back.2 = (bf16[3,640,896]{2,1,0:T(8,128)(2,1)S(1)}, f32[2,640,8]{2,1,0:T(8,128)S(1)}) custom-call(s32[1]{0:T(128)} %bitcast.10.refs_0_, s32[1]{0:T(128)} %bitcast.16.refs_1_, bf16[1280,896]{1,0:T(8,128)(2,1)S(1)} %copy-done.38, bf16[1280,896]{1,0:T(8,128)(2,1)S(1)} %copy-done.26, bf16[1280,896]{1,0:T(8,128)(2,1)S(1)} %copy-done.42, ...), custom_call_target="tpu_custom_call" | custom-call | flops 21849999360 | bytes 1024 | tf_op jit(solution)/shard_map/attend_back/pallas_call | solution.py:97
  363.5 9.5 %wgrad_qkv.2 = (bf16[640,1920]{1,0:T(8,128)(2,1)}, bf16[640,1920]{1,0:T(8,128)(2,1)}) custom-call(s32[4]{0:T(128)S(1)} %pad_add_fusion.refs_0_, s32[1]{0:T(128)} %bitcast.16.refs_1_, bf16[1280,896]{1,0:T(8,128)(2,1)S(1)} %copy-done.34, bf16[1280,896]{1,0:T(8,128)(2,1)S(1)} %copy-done.34, bf16[1280,896]{1,0:T(8,128)(2,1)S(1)} %copy-done.34, ...), custom_call_target="tpu_custom_call" | custom-call | flops 10350000128 | bytes 1024 | tf_op jit(solution)/shard_map/wgrad_qkv/pallas_call | solution.py:97
  384.1 10.8 %collective-permute-done.36.refs_9_ = bf16[160,1280]{1,0:T(8,128)(2,1)} collective-permute-done((bf16[160,1280]{1,0:T(8,128)(2,1)}, bf16[160,1280]{1,0:T(8,128)(2,1)}, u32[]{:S(2)}, u32[]{:S(2)}) %collective-permute-start.36) | collective-permute-done | bytes 409632 | tf_op jit(solution)/shard_map/ppermute | solution.py:1268
  399.7 17.1 %attend_back.3 = (bf16[3,640,896]{2,1,0:T(8,128)(2,1)S(1)}, f32[2,640,8]{2,1,0:T(8,128)S(1)}) custom-call(s32[1]{0:T(128)} %bitcast.10.refs_0_, s32[1]{0:T(128)} %bitcast.20.refs_1_, bf16[1280,896]{1,0:T(8,128)(2,1)S(1)} %copy-done.39, bf16[1280,896]{1,0:T(8,128)(2,1)S(1)} %copy-done.27, bf16[1280,896]{1,0:T(8,128)(2,1)S(1)} %copy-done.43, ...), custom_call_target="tpu_custom_call" | custom-call | flops 21849999360 | bytes 1024 | tf_op jit(solution)/shard_map/attend_back/pallas_call | solution.py:97
  419.4 9.6 %wgrad_qkv.3 = (bf16[640,1920]{1,0:T(8,128)(2,1)S(1)}, bf16[640,1920]{1,0:T(8,128)(2,1)S(1)}) custom-call(s32[4]{0:T(128)S(1)} %pad_add_fusion.1.refs_0_, s32[1]{0:T(128)} %bitcast.20.refs_1_, bf16[1280,896]{1,0:T(8,128)(2,1)S(1)} %copy-done.35, bf16[1280,896]{1,0:T(8,128)(2,1)S(1)} %copy-done.35, bf16[1280,896]{1,0:T(8,128)(2,1)S(1)} %copy-done.35, ...), custom_call_target="tpu_custom_call" | custom-call | flops 10350000128 | bytes 1024 | tf_op jit(solution)/shard_map/wgrad_qkv/pallas_call | solution.py:97
  430.7 9.2 %collective-permute-done.41.refs_0_ = bf16[160,1280]{1,0:T(8,128)(2,1)} collective-permute-done((bf16[160,1280]{1,0:T(8,128)(2,1)}, bf16[160,1280]{1,0:T(8,128)(2,1)}, u32[]{:S(2)}, u32[]{:S(2)}) %collective-permute-start.41) | collective-permute-done | bytes 409632 | tf_op jit(solution)/shard_map/ppermute | solution.py:1268
  452.3 17.1 %input_back.1 = (f32[896,1280]{1,0:T(8,128)}, f32[8,1280]{1,0:T(8,128)S(1)}) custom-call(s32[5]{0:T(128)S(1)} %stack.50.refs_0_, s32[1]{0:T(128)} %bitcast.16.refs_1_, bf16[3,640,896]{2,1,0:T(8,128)(2,1)} %copy-done.12, bf16[3,640,896]{2,1,0:T(8,128)(2,1)} %copy-done.130, f32[896,1280]{1,0:T(8,128)} %get-tuple-element.93.refs_6_.refs_4_, ...), custom_call_target="tpu_custom_call" | custom-call | flops 25300000768 | bytes 1024 | tf_op jit(solution)/shard_map/input_back/pallas_call | solution.py:97
  496.0 22.0 %down_project.1.refs_6_ = bf16[896,1280]{1,0:T(8,128)(2,1)} custom-call(s32[5]{0:T(128)S(1)} %stack.44.refs_0_, s32[1]{0:T(128)} %bitcast.4.refs_0_.refs_1_, bf16[896,5120]{1,0:T(8,128)(2,1)} %get-tuple-element.83.refs_2_.refs_5_, f32[896,1280]{1,0:T(8,128)} %get-tuple-element.82.refs_2_.refs_3_, f32[8,1280]{1,0:T(8,128)S(1)} %copy-done.140, ...), custom_call_target="tpu_custom_call" | custom-call | flops 26449999872 | bytes 1024 | tf_op jit(solution)/shard_map/down_project/pallas_call | solution.py:97
  534.4 11.9 %collective-permute-done.53.refs_7_.refs_8_ = bf16[160,1920]{1,0:T(8,128)(2,1)S(1)} collective-permute-done((bf16[160,1920]{1,0:T(8,128)(2,1)S(1)}, bf16[160,1920]{1,0:T(8,128)(2,1)S(1)}, u32[]{:S(2)}, u32[]{:S(2)}) %collective-permute-start.53) | collective-permute-done | bytes 614432 | tf_op jit(solution)/shard_map/ppermute | solution.py:1268
  555.5 11.2 %collective-permute-done.60.refs_9_ = bf16[80,1920]{1,0:T(8,128)(2,1)S(1)} collective-permute-done((bf16[80,1920]{1,0:T(8,128)(2,1)S(1)}, bf16[80,1920]{1,0:T(8,128)(2,1)S(1)}, u32[]{:S(2)}, u32[]{:S(2)}) %collective-permute-start.60) | collective-permute-done | bytes 307232 | tf_op jit(solution)/shard_map/ppermute | solution.py:1268
  567.0 10.7 %collective-permute-done.67.refs_0_ = bf16[80,640]{1,0:T(8,128)(2,1)S(1)} collective-permute-done((bf16[80,640]{1,0:T(8,128)(2,1)S(1)}, bf16[80,640]{1,0:T(8,128)(2,1)S(1)}, u32[]{:S(2)}, u32[]{:S(2)}) %collective-permute-start.67) | collective-permute-done | bytes 102432 | tf_op jit(solution)/shard_map/ppermute | solution.py:1268
  (546 shorter events, 283.9 us)
Async XLA Ops:
  83.7 42.6 %collective-permute-start.19 = (bf16[320,5120]{1,0:T(8,128)(2,1)S(1)}, bf16[320,5120]{1,0:T(8,128)(2,1)S(1)}, u32[]{:S(2)}, u32[]{:S(2)}) collective-permute-start(bf16[320,5120]{1,0:T(8,128)(2,1)S(1)} %pick.16.refs_4_), channel_id=1, source_target_pairs={{0,8},{1,17},{2,10},{3,19},{4,12},{5,21},{6,14},{7,23},{8,0},{9,25... | collective-permute-start | bytes 9830408 | tf_op jit(solution)/shard_map/ppermute | solution.py:1268
  151.6 52.7 %collective-permute-start.23 = (bf16[1280,1280]{1,0:T(8,128)(2,1)}, bf16[1280,1280]{1,0:T(8,128)(2,1)S(1)}, u32[]{:S(2)}, u32[]{:S(2)}) collective-permute-start(bf16[1280,1280]{1,0:T(8,128)(2,1)} %copy-done.5), channel_id=1, source_target_pairs={{0,8},{1,17},{2,10},{3,19},{4,12},{5,21},{6,14},{7,23},{8,0},{9,25... | collective-permute-start | bytes 9830408 | tf_op jit(solution)/shard_map/ppermute | solution.py:1268
  241.1 63.2 %collective-permute-start.29 = (bf16[1280,1280]{1,0:T(8,128)(2,1)}, bf16[1280,1280]{1,0:T(8,128)(2,1)}, u32[]{:S(2)}, u32[]{:S(2)}) collective-permute-start(bf16[1280,1280]{1,0:T(8,128)(2,1)} %copy-done.18), channel_id=1, source_target_pairs={{0,8},{1,17},{2,10},{3,19},{4,12},{5,21},{6,14},{7,23},{8,0},{9,25... | collective-permute-start | bytes 9830408 | tf_op jit(solution)/shard_map/ppermute | solution.py:1268
  277.4 27.0 %collective-permute-start.30 = (bf16[640,2560]{1,0:T(8,128)(2,1)}, bf16[640,2560]{1,0:T(8,128)(2,1)}, u32[]{:S(2)}, u32[]{:S(2)}) collective-permute-start(bf16[640,2560]{1,0:T(8,128)(2,1)} %get-tuple-element.91.refs_10_), channel_id=1, source_target_pairs={{0,1},{1,0},{2,3},{3,2},{4,5},{5,4},{6,7},{7,6},{8,9},{9,8},{10,11... | collective-permute-start | bytes 9830408 | tf_op jit(solution)/shard_map/ppermute | solution.py:1268
  277.6 26.8 %collective-permute-start.31 = (bf16[640,2560]{1,0:T(8,128)(2,1)}, bf16[640,2560]{1,0:T(8,128)(2,1)}, u32[]{:S(2)}, u32[]{:S(2)}) collective-permute-start(bf16[640,2560]{1,0:T(8,128)(2,1)} %get-tuple-element.92), channel_id=1, source_target_pairs={{0,1},{1,0},{2,3},{3,2},{4,5},{5,4},{6,7},{7,6},{8,9},{9,8},{10,11... | collective-permute-start | bytes 9830408 | tf_op jit(solution)/shard_map/ppermute | solution.py:1268
  309.1 28.5 %collective-permute-start.32 = (bf16[640,1280]{1,0:T(8,128)(2,1)S(1)}, bf16[640,1280]{1,0:T(8,128)(2,1)S(1)}, u32[]{:S(2)}, u32[]{:S(2)}) collective-permute-start(bf16[640,1280]{1,0:T(8,128)(2,1)S(1)} %combine.16.refs_9_), channel_id=1, source_target_pairs={{0,16},{1,9},{2,18},{3,11},{4,20},{5,13},{6,22},{7,15},{8,24},{9,1... | collective-permute-start | bytes 4915208 | tf_op jit(solution)/shard_map/ppermute | solution.py:1268
  325.0 52.1 %collective-permute-start.39 = (bf16[640,2560]{1,0:T(8,128)(2,1)}, bf16[640,2560]{1,0:T(8,128)(2,1)}, u32[]{:S(2)}, u32[]{:S(2)}) collective-permute-start(bf16[640,2560]{1,0:T(8,128)(2,1)} %get-tuple-element.95.refs_7_), channel_id=1, source_target_pairs={{0,8},{1,17},{2,10},{3,19},{4,12},{5,21},{6,14},{7,23},{8,0},{9,25... | collective-permute-start | bytes 9830408 | tf_op jit(solution)/shard_map/ppermute | solution.py:1268
  376.0 53.0 %collective-permute-start.42 = (bf16[640,640]{1,0:T(8,128)(2,1)}, bf16[640,640]{1,0:T(8,128)(2,1)S(1)}, u32[]{:S(2)}, u32[]{:S(2)}) collective-permute-start(bf16[640,640]{1,0:T(8,128)(2,1)} %copy-done.98), channel_id=1, source_target_pairs={{0,8},{1,17},{2,10},{3,19},{4,12},{5,21},{6,14},{7,23},{8,0},{9,25... | collective-permute-start | bytes 2457608 | tf_op jit(solution)/shard_map/ppermute | solution.py:1268
  383.0 60.0 %collective-permute-start.45 = (bf16[320,2560]{1,0:T(8,128)(2,1)}, bf16[320,2560]{1,0:T(8,128)(2,1)}, u32[]{:S(2)}, u32[]{:S(2)}) collective-permute-start(bf16[320,2560]{1,0:T(8,128)(2,1)} %combine.19.refs_12_), channel_id=1, source_target_pairs={{0,16},{1,9},{2,18},{3,11},{4,20},{5,13},{6,22},{7,15},{8,24},{9,1... | collective-permute-start | bytes 4915208 | tf_op jit(solution)/shard_map/ppermute | solution.py:1268
  419.3 27.2 %collective-permute-start.48 = (bf16[160,1280]{1,0:T(8,128)(2,1)}, bf16[160,1280]{1,0:T(8,128)(2,1)}, u32[]{:S(2)}, u32[]{:S(2)}) collective-permute-start(bf16[160,1280]{1,0:T(8,128)(2,1)} %combine.20.refs_8_.refs_1_), channel_id=1, source_target_pairs={{0,1},{1,0},{2,3},{3,2},{4,5},{5,4},{6,7},{7,6},{8,9},{9,8},{10,11... | collective-permute-start | bytes 1228808 | tf_op jit(solution)/shard_map/ppermute | solution.py:1268
  440.7 34.6 %collective-permute-start.47 = (bf16[640,1920]{1,0:T(8,128)(2,1)}, bf16[640,1920]{1,0:T(8,128)(2,1)S(1)}, u32[]{:S(2)}, u32[]{:S(2)}) collective-permute-start(bf16[640,1920]{1,0:T(8,128)(2,1)} %copy-done.77), channel_id=1, source_target_pairs={{0,8},{1,17},{2,10},{3,19},{4,12},{5,21},{6,14},{7,23},{8,0},{9,25... | collective-permute-start | bytes 7372808 | tf_op jit(solution)/shard_map/ppermute | solution.py:1268
  441.9 40.7 %collective-permute-start.44 = (bf16[320,640]{1,0:T(8,128)(2,1)}, bf16[320,640]{1,0:T(8,128)(2,1)}, u32[]{:S(2)}, u32[]{:S(2)}) collective-permute-start(bf16[320,640]{1,0:T(8,128)(2,1)} %copy-done.104), channel_id=1, source_target_pairs={{0,16},{1,9},{2,18},{3,11},{4,20},{5,13},{6,22},{7,15},{8,24},{9,1... | collective-permute-start | bytes 1228808 | tf_op jit(solution)/shard_map/ppermute | solution.py:1268
  443.0 40.8 %collective-permute-start.40 = (bf16[160,1280]{1,0:T(8,128)(2,1)}, bf16[160,1280]{1,0:T(8,128)(2,1)}, u32[]{:S(2)}, u32[]{:S(2)}) collective-permute-start(bf16[160,1280]{1,0:T(8,128)(2,1)} %combine.20.refs_8_.refs_1_), channel_id=1, source_target_pairs={{0,2},{1,3},{2,0},{3,1},{4,6},{5,7},{6,4},{7,5},{8,10},{9,11},{10,... | collective-permute-start | bytes 1228808 | tf_op jit(solution)/shard_map/ppermute | solution.py:1268
  446.6 37.3 %collective-permute-start.43 = (bf16[160,1280]{1,0:T(8,128)(2,1)}, bf16[160,1280]{1,0:T(8,128)(2,1)}, u32[]{:S(2)}, u32[]{:S(2)}) collective-permute-start(bf16[160,1280]{1,0:T(8,128)(2,1)} %land.34.refs_6_.refs_2_), channel_id=1, source_target_pairs={{0,2},{1,3},{2,0},{3,1},{4,6},{5,7},{6,4},{7,5},{8,10},{9,11},{10,... | collective-permute-start | bytes 1228808 | tf_op jit(solution)/shard_map/ppermute | solution.py:1268
  448.7 32.2 %collective-permute-start.46 = (bf16[160,2560]{1,0:T(8,128)(2,1)S(1)}, bf16[160,2560]{1,0:T(8,128)(2,1)S(1)}, u32[]{:S(2)}, u32[]{:S(2)}) collective-permute-start(bf16[160,2560]{1,0:T(8,128)(2,1)S(1)} %combine.22.refs_24_), channel_id=1, source_target_pairs={{0,2},{1,3},{2,0},{3,1},{4,6},{5,7},{6,4},{7,5},{8,10},{9,11},{10,... | collective-permute-start | bytes 2457608 | tf_op jit(solution)/shard_map/ppermute | solution.py:1268
  485.0 33.0 %collective-permute-start.52 = (bf16[320,1920]{1,0:T(8,128)(2,1)}, bf16[320,1920]{1,0:T(8,128)(2,1)S(1)}, u32[]{:S(2)}, u32[]{:S(2)}) collective-permute-start(bf16[320,1920]{1,0:T(8,128)(2,1)} %copy-done.79), channel_id=1, source_target_pairs={{0,16},{1,9},{2,18},{3,11},{4,20},{5,13},{6,22},{7,15},{8,24},{9,1... | collective-permute-start | bytes 3686408 | tf_op jit(solution)/shard_map/ppermute | solution.py:1268
  485.9 35.7 %collective-permute-start.58 = (bf16[80,2560]{1,0:T(8,128)(2,1)}, bf16[80,2560]{1,0:T(8,128)(2,1)S(1)}, u32[]{:S(2)}, u32[]{:S(2)}) collective-permute-start(bf16[80,2560]{1,0:T(8,128)(2,1)} %copy-done.101), channel_id=1, source_target_pairs={{0,4},{1,5},{2,6},{3,7},{4,0},{5,1},{6,2},{7,3},{8,12},{9,13},{10,... | collective-permute-start | bytes 1228808 | tf_op jit(solution)/shard_map/ppermute | solution.py:1268
  485.9 38.5 %collective-permute-start.57 = (bf16[160,640]{1,0:T(8,128)(2,1)S(1)}, bf16[160,640]{1,0:T(8,128)(2,1)S(1)}, u32[]{:S(2)}, u32[]{:S(2)}) collective-permute-start(bf16[160,640]{1,0:T(8,128)(2,1)S(1)} %combine.25.refs_2_), channel_id=1, source_target_pairs={{0,2},{1,3},{2,0},{3,1},{4,6},{5,7},{6,4},{7,5},{8,10},{9,11},{10,... | collective-permute-start | bytes 614408 | tf_op jit(solution)/shard_map/ppermute | solution.py:1268
  493.7 33.6 %collective-permute-start.54 = (f32[1,3968]{1,0:T(1,128)S(1)}, f32[1,3968]{1,0:T(1,128)S(1)}, u32[]{:S(2)}, u32[]{:S(2)}) collective-permute-start(f32[1,3968]{1,0:T(1,128)S(1)} %get-tuple-element.117), channel_id=1, source_target_pairs={{0,8},{1,9},{2,10},{3,11},{4,12},{5,13},{6,14},{7,15},{8,0},{9,1},... | collective-permute-start | bytes 47624 | tf_op jit(solution)/shard_map/ppermute | solution.py:1268
  495.1 32.3 %collective-permute-start.55 = (f32[1,3968]{1,0:T(1,128)S(1)}, f32[1,3968]{1,0:T(1,128)S(1)}, u32[]{:S(2)}, u32[]{:S(2)}) collective-permute-start(f32[1,3968]{1,0:T(1,128)S(1)} %get-tuple-element.118), channel_id=1, source_target_pairs={{0,16},{1,17},{2,18},{3,19},{4,20},{5,21},{6,22},{7,23},{8,24},{9,... | collective-permute-start | bytes 47624 | tf_op jit(solution)/shard_map/ppermute | solution.py:1268
  524.4 26.0 %collective-permute-start.62 = (bf16[80,2560]{1,0:T(8,128)(2,1)S(1)}, bf16[80,2560]{1,0:T(8,128)(2,1)S(1)}, u32[]{:S(2)}, u32[]{:S(2)}) collective-permute-start(bf16[80,2560]{1,0:T(8,128)(2,1)S(1)} %combine.27.refs_8_.refs_1_), channel_id=1, source_target_pairs={{0,4},{1,5},{2,6},{3,7},{4,0},{5,1},{6,2},{7,3},{8,12},{9,13},{10,... | collective-permute-start | bytes 1228808 | tf_op jit(solution)/shard_map/ppermute | solution.py:1268
  527.3 25.5 %collective-permute-start.61 = (bf16[80,2560]{1,0:T(8,128)(2,1)S(1)}, bf16[80,2560]{1,0:T(8,128)(2,1)S(1)}, u32[]{:S(2)}, u32[]{:S(2)}) collective-permute-start(bf16[80,2560]{1,0:T(8,128)(2,1)S(1)} %combine.27.refs_8_.refs_1_), channel_id=1, source_target_pairs={{0,1},{1,0},{2,3},{3,2},{4,5},{5,4},{6,7},{7,6},{8,9},{9,8},{10,11... | collective-permute-start | bytes 1228808 | tf_op jit(solution)/shard_map/ppermute | solution.py:1268
  550.5 27.2 %collective-permute-start.69 = (bf16[80,2560]{1,0:T(8,128)(2,1)S(1)}, bf16[80,2560]{1,0:T(8,128)(2,1)S(1)}, u32[]{:S(2)}, u32[]{:S(2)}) collective-permute-start(bf16[80,2560]{1,0:T(8,128)(2,1)S(1)} %combine.27.refs_8_.refs_1_), channel_id=1, source_target_pairs={{0,2},{1,3},{2,0},{3,1},{4,6},{5,7},{6,4},{7,5},{8,10},{9,11},{10,... | collective-permute-start | bytes 1228808 | tf_op jit(solution)/shard_map/ppermute | solution.py:1268
  552.8 27.3 %collective-permute-start.70 = (bf16[80,2560]{1,0:T(8,128)(2,1)S(1)}, bf16[80,2560]{1,0:T(8,128)(2,1)S(1)}, u32[]{:S(2)}, u32[]{:S(2)}) collective-permute-start(bf16[80,2560]{1,0:T(8,128)(2,1)S(1)} %land.36.refs_2_), channel_id=1, source_target_pairs={{0,2},{1,3},{2,0},{3,1},{4,6},{5,7},{6,4},{7,5},{8,10},{9,11},{10,... | collective-permute-start | bytes 1228808 | tf_op jit(solution)/shard_map/ppermute | solution.py:1268
  (213 other events, 1608.1 us)
